TPU v7x, 512 devices: a whole 4x8x8 slice. The times are simulated.
512 devices in a mesh: rep: 16 (over x, y_hi), fsdp: 32 (over z, y_lo, core).
Axes of the slice: x: 4, y: 8 (y_hi: 4, y_lo: 2; y = y_hi * 2 + y_lo), z: 8, core: 2. Of those that a mesh axis runs over, the one named last changes fastest.
Arguments:
- tokens: bfloat16 [16, 4096, 8192], P('rep', 'fsdp'), may hold values from -6 to 6
- cotangent: bfloat16 [16, 4096, 512], P('rep', 'fsdp'), may hold values from -6 to 6
- weight: bfloat16 [16, 8192, 512], P('rep', 'fsdp'), may hold values from -6 to 6
- moment: float32 [16, 8192, 512], P('rep', 'fsdp'), may hold values from -6 to 6
- global_frag: float32 [2, 8192, 128], P(None, 'fsdp'), may hold values from -6 to 6
- outer_moment: float32 [2, 8192, 128], P(None, 'fsdp'), may hold values from -3 to 3
- fragment: int32 [4], replicated, may hold values from 0 to 3, each once
Outputs:
- key_out: bfloat16 [16, 4096, 512], P('rep', 'fsdp')
- moment_new: float32 [16, 8192, 512], P('rep', 'fsdp')
- weight_new: bfloat16 [16, 8192, 512], P('rep', 'fsdp')
- global_new: float32 [2, 8192, 128], P(None, 'fsdp')
- outer_new: float32 [2, 8192, 128], P(None, 'fsdp')
Inputs may be any that keep to these rules, and one draw needn't show every extreme that they name: `fragment`: each head appears once.
All inputs are finite; a program needn't handle non-finite values.
Results may differ from a plain program's by a relative error of at most 0.001.
Values may be sent and summed in bfloat16 or wider, within the bound.
No kernel may reach another device: no remote copies, remote signals or barrier semaphores. Data moves between devices by JAX's collectives and lax.ppermute only.
A program may use at most 64 MiB of HBM per device.

v0:
```python
import jax
import jax.numpy as jnp
from jax import lax
from jax.sharding import PartitionSpec as P

D = 8192
HD = 128
KVH = 4


LR_INNER = 0.1
BETA_INNER = 0.9
MU_OUTER = 0.9
LR_OUTER = 0.7
ALPHA_MIX = 0.5


def shards(tokens, cotangent, weight, moment, global_frag, outer_moment, fragment):
    scale_factor = D ** (-0.5)
    width = weight.shape[2]
    local_tokens = tokens[0]
    key_sum = jnp.dot(
        local_tokens,
        lax.all_gather(weight, "fsdp", axis=1, tiled=True)[0],
        preferred_element_type=jnp.float32,
    )
    key_out = (key_sum * scale_factor).astype(jnp.bfloat16)[None]
    feature_cols = lax.all_to_all(tokens, "fsdp", split_axis=2, concat_axis=1, tiled=True)[0]
    grad_sum = lax.dot_general(
        feature_cols,
        lax.all_gather(cotangent, "fsdp", axis=1, tiled=True)[0],
        (((0,), (0,)), ((), ())),
        preferred_element_type=jnp.float32,
    )
    moment_new = BETA_INNER * moment[0] + grad_sum * scale_factor
    inner = weight[0].astype(jnp.float32) - LR_INNER * moment_new
    head_first = fragment[0]
    head_second = fragment[1]
    prev_first = lax.dynamic_slice_in_dim(weight[0], head_first * HD, HD, 1).astype(jnp.float32)
    prev_second = lax.dynamic_slice_in_dim(weight[0], head_second * HD, HD, 1).astype(jnp.float32)
    delta = global_frag - jnp.stack([prev_first, prev_second], axis=0)
    delta_total = lax.psum(delta, "rep")
    mean_delta = delta_total / lax.axis_size("rep")
    outer_new = MU_OUTER * outer_moment + mean_delta
    global_new = global_frag - LR_OUTER * (MU_OUTER * outer_new + mean_delta)
    column_head = lax.broadcasted_iota(jnp.int32, (1, width), 1) // HD
    spread_first = jnp.tile(global_new[0], (1, KVH))
    spread_second = jnp.tile(global_new[1], (1, KVH))
    merged = jnp.where(
        column_head == head_first,
        ALPHA_MIX * inner + (1.0 - ALPHA_MIX) * spread_first,
        jnp.where(
            column_head == head_second, ALPHA_MIX * inner + (1.0 - ALPHA_MIX) * spread_second, inner
        ),
    )
    return (key_out, moment_new[None], merged.astype(jnp.bfloat16)[None], global_new, outer_new)


def solution(mesh):
    in_specs = (
        P("rep", "fsdp", None),
        P("rep", "fsdp", None),
        P("rep", "fsdp", None),
        P("rep", "fsdp", None),
        P(None, "fsdp", None),
        P(None, "fsdp", None),
        P(),
    )
    out_specs = (
        P("rep", "fsdp", None),
        P("rep", "fsdp", None),
        P("rep", "fsdp", None),
        P(None, "fsdp", None),
        P(None, "fsdp", None),
    )
    return jax.shard_map(shards, mesh=mesh, in_specs=in_specs, out_specs=out_specs, check_vma=False)
```

profile of v0, /device:TPU:8, one launch (start us, length us, event | category | flops | bytes accessed | tf_op | source)
XLA Modules:
  0.0 225.7 jit_solution(13361287836439369610)
XLA Ops:
  8.0 1.3 fusion.37
  10.7 0.9 constant_dynamic-slice_fusion.1
  11.6 1.7 convert_subtract_fusion.1
  13.3 0.0 all-gather.5.cloned.1.call-start
  13.3 0.5 all-gather.5.cloned.1.call-update
  13.8 0.0 all-gather.3.cloned.1.call-start
  13.9 0.5 all-gather.3.cloned.1.call-update
  14.4 9.5 %copy.14 = bf16[1,128,8192]{1,0,2:T(2,128)(2,1)} copy(bf16[1,128,8192]{2,1,0:T(8,128)(2,1)} %param.7) | data formatting | bytes 4194304 | tf_op args[0]
  23.9 0.5 broadcast.102
  24.4 45.2 %reduce = bf16[8192,128]{1,0:T(8,128)(2,1)S(1)} reduce(bf16[8192,1,128]{2,1,0:T(2,128)(2,1)} %bitcast.68, bf16[]{:T(256)} %broadcast.102), dimensions={1}, to_apply=%bitcast.65.reduce_sub_computation | reduce | bytes 4194306
  69.6 2.1 reshape.76
  71.7 12.1 %all-to-all-start = ((bf16[32,2,16384]{2,1,0:T(2,128)(2,1)}), bf16[32,2,16384]{2,1,0:T(2,128)(2,1)S(1)}, u32[]{:S(2)}, u32[]{:S(2)}) async-start(bf16[32,2,16384]{2,1,0:T(2,128)(2,1)} %reshape.76), calls=%async_computation | async-start | bytes 4194304 | tf_op jit(solution)/shard_map/all_to_all | solution.py:28
  83.8 1.3 fusion.34
  85.1 107.7 %all-reduce.2.cloned.1.call-done = f32[2,256,128]{2,1,0:T(8,128)} async-done(((f32[2,256,128]{2,1,0:T(8,128)}), f32[2,256,128]{2,1,0:T(8,128)}) %all-reduce.2.cloned.1.call-update) | async-done | bytes 262160 | tf_op jit(solution)/shard_map/psum | solution.py:42
  192.8 1.7 multiply_subtract_fusion
  194.6 6.8 %reshape.77 = bf16[8192,1,128]{2,1,0:T(2,128)(2,1)} reshape(bf16[32,2,16384]{2,1,0:T(2,128)(2,1)S(1)} %all-to-all-done) | data formatting | bytes 4194304
  201.4 2.5 %copy.16 = bf16[1,128,8192]{1,2,0:T(8,128)(2,1)S(1)} copy(bf16[1,128,8192]{1,0,2:T(2,128)(2,1)} %bitcast.69) | data formatting | bytes 4194304
  203.8 3.0 %copy.15 = bf16[1,32,128,256]{3,2,1,0:T(8,128)(2,1)} copy(bf16[1,32,128,256]{2,3,1,0:T(8,128)(2,1)S(1)} %bitcast.70) | data formatting | bytes 4194304 | tf_op jit(solution)/shard_map/all_to_all | solution.py:28
  206.8 4.2 %fusion.8 = f32[256,512]{1,0:T(8,128)S(1)} fusion(bf16[4096,256]{1,0:T(8,128)(2,1)} %bitcast.71, bf16[1,4096,512]{2,1,0:T(8,128)(2,1)} %all-gather.5.cloned.1.call-done, f32[1,256,512]{2,1,0:T(8,128)} %param.10), kind=kOutput, calls=%fused_computation.6 | convolution fusion | flops 1074135040 | bytes 7340032 | tf_op jit(solution)/shard_map/dot_general | solution.py:29
  211.1 0.1 tile.5
  211.2 0.1 tile.4
  211.3 0.9 fusion.29
  212.2 0.7 copy-done
  212.9 5.3 %fusion.21 = bf16[1,128,512]{2,1,0:T(8,128)(2,1)} fusion(bf16[1,8192,512]{2,1,0:T(8,128)(2,1)} %all-gather.3.cloned.1.call-done, bf16[1,128,8192]{2,1,0:T(8,128)(2,1)S(1)} %copy-done), kind=kOutput, calls=%fused_computation.9 | convolution fusion | flops 1073872896 | bytes 10616832 | tf_op jit(solution)/shard_map/dot_general | solution.py:22
  (17 shorter events, 0.1 us)
Async XLA Ops:
  8.0 184.8 %all-reduce.2.cloned.1.call-start = ((), (), s32[]{:S(2)}) async-start(), calls=%async_computation.3 | async-start | bytes 524288 | tf_op jit(solution)/shard_map/psum | solution.py:42
  13.3 193.6 %all-gather.5.cloned.1.call-start = ((), (), s32[]{:S(2)}) async-start(), calls=%async_computation.2 | async-start | bytes 4325376 | tf_op jit(solution)/shard_map/all_gather | solution.py:31
  13.8 198.4 %all-gather.3.cloned.1.call-start = ((), (), s32[]{:S(2)}) async-start(), calls=%async_computation.1 | async-start | bytes 8650752 | tf_op jit(solution)/shard_map/all_gather | solution.py:24
  71.7 121.1 %copy-start.2 = (f32[2,256,128]{2,1,0:T(8,128)S(1)}, f32[2,256,128]{2,1,0:T(8,128)}, u32[]{:S(2)}) copy-start(f32[2,256,128]{2,1,0:T(8,128)} %param.11) | copy-start | bytes 786436
  71.7 121.1 %copy-start.5 = (f32[2,256,128]{2,1,0:T(8,128)S(1)}, f32[2,256,128]{2,1,0:T(8,128)}, u32[]{:S(2)}) copy-start(f32[2,256,128]{2,1,0:T(8,128)} %param.12) | copy-start | bytes 786436
  71.7 122.9 %all-to-all-start = ((bf16[32,2,16384]{2,1,0:T(2,128)(2,1)}), bf16[32,2,16384]{2,1,0:T(2,128)(2,1)S(1)}, u32[]{:S(2)}, u32[]{:S(2)}) async-start(bf16[32,2,16384]{2,1,0:T(2,128)(2,1)} %reshape.76), calls=%async_computation | async-start | bytes 4194304 | tf_op jit(solution)/shard_map/all_to_all | solution.py:28
  194.5 6.8 %copy-start.3 = (f32[2,256,128]{2,1,0:T(8,128)}, f32[2,256,128]{2,1,0:T(8,128)S(1)}, u32[]{:S(2)}) copy-start(f32[2,256,128]{2,1,0:T(8,128)S(1)} %get-tuple-element.5) | copy-start | bytes 786436
  206.8 4.5 %copy-start.1 = (bf16[1,256,512]{2,1,0:T(8,128)(2,1)S(1)}, bf16[1,256,512]{2,1,0:T(8,128)(2,1)}, u32[]{:S(2)}) copy-start(bf16[1,256,512]{2,1,0:T(8,128)(2,1)} %param.9) | copy-start | bytes 786436
  211.1 7.2 %copy-start.4 = (f32[256,512]{1,0:T(8,128)}, f32[256,512]{1,0:T(8,128)S(1)}, u32[]{:S(2)}) copy-start(f32[256,512]{1,0:T(8,128)S(1)} %fusion.8) | copy-start | bytes 1572868
  211.1 1.9 copy-start
Sparse Core Ops, SparseCore 0:
  13.4 179.3 all-reduce.1
Sparse Core Ops, SparseCore 1:
  15.9 101.2 all-gather.4
  119.2 77.7 all-gather.2
where the time goes:
time: 226 us
  waiting for transfers between devices  109 us (48%)
  other arithmetic  50.8 us (22%)
  local copies, waits for them, and re-layouts  27.5 us (12%)
  between operations  16.9 us (7%)
  starting transfers between devices  12.2 us (5%)
  matrix products  9.51 us (4%)
    psum x1, waiting for transfers between devices, shards(): delta_total = lax.psum(delta, 'rep')  108 us
    unnamed x1, other arithmetic  45.2 us
    unnamed x17, local copies, waits for them, and re-layouts  22.1 us
    all_to_all x1, starting transfers between devices, shards(): lax.all_to_all(tokens, 'fsdp', split_axis=2, concat_axis=1, tiled=True)[0]  12.1 us
    dot_general x1, matrix products, shards(): jnp.dot(local_tokens, lax.all_gather(weight, 'fsdp', axis=1, tiled=True)[...  5.3 us
  transfers between devices with their start and end apart: 4, of which 1 were waited for; matrix products, arithmetic and copies ran while one was open for 35% of the time, Pallas kernels for 0%

commit v1 on v0

v1 whole, which is shorter than its diff:
```python
import functools

import jax
import jax.numpy as jnp
from jax import lax
from jax.experimental import pallas as pl
from jax.experimental.pallas import tpu as pltpu
from jax.sharding import PartitionSpec as P

D = 8192
HD = 128
KVH = 4

LR_INNER = 0.1
BETA_INNER = 0.9
MU_OUTER = 0.9
LR_OUTER = 0.7
ALPHA_MIX = 0.5

F32 = jnp.float32
BF16 = jnp.bfloat16

NZ, NY, NC = 8, 2, 2
NG = NY * NC

ROWS = 256
TOK = 128
EARLY = (4, 3, -3)
LATE = (2, -2, 1, -1, 0)
DIST = EARLY + LATE
SPLIT = len(EARLY) * ROWS + KVH * HD
WIDE = SPLIT + len(LATE) * ROWS
LEVELS = 32000.0
CODED = ROWS + 16


def place(z, y, c):
    return ((z % NZ) * NY + y) * NC + c


def ring(dist):
    return [
        (place(z, y, c), place(z + (dist if c == 0 else -dist), y, c))
        for z in range(NZ) for y in range(NY) for c in range(NC)
    ]


def swap(k):
    return [(f, f ^ k) for f in range(NZ * NG)]


def z_groups():
    return [[place(z, y, c) for z in range(NZ)] for y in range(NY) for c in range(NC)]


def owner(dist, k=0):
    me = lax.axis_index("fsdp")
    z = me // NG
    forward = 1 - 2 * ((me % NC) ^ (k % NC))
    return (z + forward * dist + NZ) % NZ


def column_of(i):
    first = 0 if i < len(EARLY) else KVH * HD
    return first + i * ROWS


def piece_of(tok, i, k):
    me = lax.axis_index("fsdp")
    block = owner(DIST[i], k) * NG + ((me % NG) ^ k)
    return tok.at[:, pl.ds(pl.multiple_of(block * ROWS, ROWS), ROWS)]


def copy_all(pairs, sems):
    copies = [pltpu.make_async_copy(src, dst, sems.at[n]) for n, (src, dst) in enumerate(pairs)]
    for copy in copies:
        copy.start()
    for copy in copies:
        copy.wait()


def pack_early_kernel(tok, cot, y_early, x_early, near, sems):
    pairs = []
    for out, k in ((y_early, 2), (x_early, 3), (near, 1)):
        for i in range(len(DIST) if k == 1 else len(EARLY)):
            pairs.append((piece_of(tok, i, k), out.at[:, pl.ds(column_of(i), ROWS)]))
        pairs.append((cot, out.at[:, pl.ds(SPLIT - KVH * HD, KVH * HD)]))
    copy_all(pairs, sems)


def pack_late_kernel(frag, tok, cot, w, y_late, x_late, own, picked, sems):
    pairs = []
    for out, k in ((y_late, 2), (x_late, 3)):
        for i in range(len(EARLY), len(DIST)):
            pairs.append((piece_of(tok, i, k), out.at[:, pl.ds(column_of(i) - SPLIT, ROWS)]))
    for i in range(len(DIST)):
        pairs.append((piece_of(tok, i, 0), own.at[:, pl.ds(column_of(i), ROWS)]))
    pairs.append((cot, own.at[:, pl.ds(SPLIT - KVH * HD, KVH * HD)]))
    for k in range(2):
        src = w.at[:, pl.ds(pl.multiple_of(frag[k] * HD, HD), HD)]
        pairs.append((src, picked.at[:, pl.ds(k * HD, HD)]))
    copy_all(pairs, sems)


def encode(x, out):
    top = jnp.max(jnp.abs(x), axis=0, keepdims=True)
    power = jnp.ceil(jnp.log2(jnp.maximum(top, 1e-30)))
    out[:ROWS, :] = jnp.round(x * (LEVELS * jnp.exp2(-power))).astype(jnp.int32).astype(jnp.int16)
    out[ROWS:, :] = jnp.broadcast_to(power, (CODED - ROWS, x.shape[1])).astype(jnp.int32).astype(jnp.int16)


def decode(ref):
    power = ref[ROWS:, :].astype(jnp.int32).astype(F32)[0:1]
    return ref[:ROWS, :].astype(jnp.int32).astype(F32) * (jnp.exp2(power) * (1.0 / LEVELS))


def partial_grad(columns, cot):
    features = jnp.concatenate(columns, axis=0)
    return lax.dot_general(features, cot, (((0,), (0,)), ((), ())), preferred_element_type=F32)


def cotangents(refs):
    return jnp.concatenate([r[:, SPLIT - KVH * HD : SPLIT] for r in refs], axis=0)


def early_kernel(own, near, y_early, x_early, *outs):
    refs = (own, near, y_early, x_early)
    cot = cotangents(refs)
    for i, out in enumerate(outs):
        at = column_of(i)
        encode(partial_grad([r[:, at : at + ROWS] for r in refs], cot), out)


def late_columns(own, near, y_late, x_late, dist):
    at = column_of(DIST.index(dist))
    return [own[:, at : at + ROWS], near[:, at : at + ROWS],
            y_late[:, at - SPLIT : at - SPLIT + ROWS], x_late[:, at - SPLIT : at - SPLIT + ROWS]]


def next_kernel(own, near, y_early, x_early, y_late, x_late, ahead, behind, here):
    cot = cotangents((own, near, y_early, x_early))
    encode(partial_grad(late_columns(own, near, y_late, x_late, 1), cot), ahead)
    encode(partial_grad(late_columns(own, near, y_late, x_late, -1), cot), behind)
    here[...] = partial_grad(late_columns(own, near, y_late, x_late, 0), cot)


def relay_kernel(own, near, y_early, x_early, y_late, x_late, from4, from3, back3, ahead, behind):
    cot = cotangents((own, near, y_early, x_early))
    forward = partial_grad(late_columns(own, near, y_late, x_late, 2), cot)
    encode(forward + decode(from4) + decode(from3), ahead)
    backward = partial_grad(late_columns(own, near, y_late, x_late, -2), cot)
    encode(backward + decode(back3), behind)


def key_kernel(own, near, y_early, x_early, y_late, x_late, w, *outs):
    for k, (first, second) in enumerate(((own, None), (near, None), (y_early, y_late), (x_early, x_late))):
        total = jnp.zeros((TOK, KVH * HD), F32)
        for i, dist in enumerate(DIST):
            at = column_of(i)
            if second is None or at < SPLIT:
                piece = first[:, at : at + ROWS]
            else:
                piece = second[:, at - SPLIT : at - SPLIT + ROWS]
            rows = w[pl.ds(pl.multiple_of(owner(dist) * ROWS, ROWS), ROWS), :]
            total = total + jnp.dot(piece, rows, preferred_element_type=F32)
        outs[k][...] = total


def update_kernel(frag, here, ahead2, behind2, ahead1, behind1, w, moment, picked_sum, gf, om,
                  moment_new, weight_new, global_new, outer_new, *, replicas):
    grad = here[...] + decode(ahead2) + decode(behind2) + decode(ahead1) + decode(behind1)
    new = BETA_INNER * moment[...] + grad * (D ** -0.5)
    moment_new[...] = new
    inner = w[...].astype(F32) - LR_INNER * new
    for k in range(2):
        mean = gf[k] - picked_sum[:, k * HD : (k + 1) * HD] * (1.0 / replicas)
        out = MU_OUTER * om[k] + mean
        outer_new[k] = out
        global_new[k] = gf[k] - LR_OUTER * (MU_OUTER * out + mean)
    for h in range(KVH):
        mine = inner[:, h * HD : (h + 1) * HD]
        first = ALPHA_MIX * mine + (1.0 - ALPHA_MIX) * global_new[0]
        second = ALPHA_MIX * mine + (1.0 - ALPHA_MIX) * global_new[1]
        merged = jnp.where(frag[0] == h, first, jnp.where(frag[1] == h, second, mine))
        weight_new[:, h * HD : (h + 1) * HD] = merged.astype(BF16)


def key_sum_kernel(a, b, c, d, out):
    out[...] = ((a[...] + b[...] + c[...] + d[...]) * (D ** -0.5)).astype(BF16)


def call(kernel, outs, *args, flops=0, scalars=0, copies=0):
    moved = sum(a.size * a.dtype.itemsize for a in args)
    moved += sum(o.size * o.dtype.itemsize for o in outs)
    space = pl.ANY if copies else pltpu.VMEM
    specs = [pl.BlockSpec(memory_space=pltpu.SMEM)] * scalars
    specs += [pl.BlockSpec(memory_space=space)] * (len(args) - scalars)
    return pl.pallas_call(
        kernel,
        out_shape=list(outs),
        in_specs=specs,
        out_specs=[pl.BlockSpec(memory_space=pltpu.VMEM)] * len(outs),
        scratch_shapes=[pltpu.SemaphoreType.DMA((copies,))] if copies else [],
        compiler_params=None if copies else pltpu.CompilerParams(vmem_limit_bytes=24 * 2**20),
        cost_estimate=pl.CostEstimate(flops=0, bytes_accessed=0, transcendentals=0),
    )(*args)


def shape(*dims, kind=BF16):
    return jax.ShapeDtypeStruct(dims, kind)


def shards(tokens, cotangent, weight, moment, global_frag, outer_moment, fragment):
    replicas = lax.axis_size("rep")
    width = KVH * HD
    w = weight[0]
    w_rows = lax.all_gather(w, "fsdp", axis_index_groups=z_groups(), tiled=True)

    send = lambda x, pairs: lax.ppermute(x, "fsdp", pairs)
    y_early, x_early, near = call(
        pack_early_kernel, [shape(TOK, SPLIT)] * 2 + [shape(TOK, WIDE)], tokens[0], cotangent[0],
        copies=2 * len(EARLY) + len(DIST) + 3,
    )
    y_early = send(y_early, swap(2))
    x_early = send(x_early, swap(3))
    near = send(near, swap(1))
    y_late, x_late, own, picked = call(
        pack_late_kernel,
        [shape(TOK, WIDE - SPLIT)] * 2 + [shape(TOK, WIDE), shape(ROWS, 2 * HD)],
        fragment, tokens[0], cotangent[0], w, scalars=1, copies=2 * len(LATE) + len(DIST) + 3,
    )
    y_late = send(y_late, swap(2))
    x_late = send(x_late, swap(3))

    share = lax.all_to_all(picked.reshape(replicas, ROWS // replicas, 2 * HD), "rep", 0, 0)
    summed = jnp.sum(share.astype(F32), axis=0)
    coded = shape(CODED, width, kind=jnp.int16)
    block_flops = 2 * NG * TOK * ROWS * width
    to4, to3, back3 = call(early_kernel, [coded] * 3, own, near, y_early, x_early, flops=3 * block_flops)
    from4 = send(to4, ring(2))
    from3 = send(to3, ring(1))
    back3 = send(back3, ring(-1))

    got = (own, near, y_early, x_early, y_late, x_late)
    ahead1, behind1, here = call(
        next_kernel, [coded, coded, shape(ROWS, width, kind=F32)], *got, flops=3 * block_flops
    )
    picked_sum = lax.all_to_all(
        jnp.broadcast_to(summed[None], (replicas,) + summed.shape), "rep", 0, 0
    ).reshape(ROWS, 2 * HD)
    ahead1 = send(ahead1, ring(1))
    behind1 = send(behind1, ring(-1))
    ahead2, behind2 = call(relay_kernel, [coded] * 2, *got, from4, from3, back3, flops=2 * block_flops)
    ahead2 = send(ahead2, ring(2))
    behind2 = send(behind2, ring(-2))

    parts = call(key_kernel, [shape(TOK, width, kind=F32)] * NG, *got, w_rows, flops=8 * block_flops)
    (key_out,) = call(
        key_sum_kernel, [shape(TOK, width)], parts[0], *[send(parts[k], swap(k)) for k in range(1, NG)]
    )

    moment_new, weight_new, global_new, outer_new = call(
        functools.partial(update_kernel, replicas=replicas),
        [shape(ROWS, width, kind=F32), shape(ROWS, width), shape(2, ROWS, HD, kind=F32), shape(2, ROWS, HD, kind=F32)],
        fragment, here, ahead2, behind2, ahead1, behind1, w, moment[0], picked_sum, global_frag, outer_moment,
        scalars=1,
    )
    return key_out[None], moment_new[None], weight_new[None], global_new, outer_new


def solution(mesh):
    in_specs = (
        P("rep", "fsdp", None),
        P("rep", "fsdp", None),
        P("rep", "fsdp", None),
        P("rep", "fsdp", None),
        P(None, "fsdp", None),
        P(None, "fsdp", None),
        P(),
    )
    out_specs = (
        P("rep", "fsdp", None),
        P("rep", "fsdp", None),
        P("rep", "fsdp", None),
        P(None, "fsdp", None),
        P(None, "fsdp", None),
    )
    return jax.shard_map(shards, mesh=mesh, in_specs=in_specs, out_specs=out_specs, check_vma=False)
```

time: 226 us -> 116 us (0.51)
  the two profiles are of different devices: /device:TPU:8 before, /device:TPU:1 now
where the time goes in v1:
time: 116 us; the launch traced here: 115 us
  starting transfers between devices  70.4 us (61%)
  Pallas kernels  16.9 us (15%)
  between operations  14.3 us (12%)
  local copies, waits for them, and re-layouts  8.88 us (8%)
  waiting for transfers between devices  4.72 us (4%)
    ppermute x15, starting transfers between devices, shards(): send = lambda x, pairs: lax.ppermute(x, 'fsdp', pairs)  57.3 us
    pallas_call x8, Pallas kernels, call(): pl.pallas_call(kernel, out_shape=list(outs), in_specs=specs, out_specs=[p...  16.9 us
    all_to_all x1, starting transfers between devices, shards(): lax.all_to_all(jnp.broadcast_to(summed[None], (replicas,) + summed.shape)...  9.07 us
    unnamed x24, local copies, waits for them, and re-layouts  8.15 us
    all_to_all x1, starting transfers between devices, shards(): lax.all_to_all(picked.reshape(replicas, ROWS // replicas, 2 * HD), 'rep',...  4.02 us
    ppermute x15, waiting for transfers between devices, shards(): send = lambda x, pairs: lax.ppermute(x, 'fsdp', pairs)  4.01 us
  transfers between devices with their start and end apart: 18, of which 2 were waited for; matrix products, arithmetic and copies ran while one was open for 1% of the time, Pallas kernels for 14%

profile of v1, /device:TPU:1, one launch (start us, length us, event | category | flops | bytes accessed | tf_op | source)
XLA Modules:
  0.0 115.3 jit_solution(15161065671411974031)
XLA Ops:
  7.9 2.7 %shard_map.111 = (bf16[128,1280]{1,0:T(8,128)(2,1)}, bf16[128,1280]{1,0:T(8,128)(2,1)}, bf16[128,2560]{1,0:T(8,128)(2,1)}) custom-call(bf16[128,8192]{1,0:T(8,128)(2,1)} %bitcast.15, bf16[128,512]{1,0:T(8,128)(2,1)} %bitcast.17), custom_call_target="tpu_custom_call" | custom-call | tf_op jit(solution)/shard_map/pallas_call | solution.py:198
  10.6 8.8 %collective-permute-start = (bf16[128,2560]{1,0:T(8,128)(2,1)}, bf16[128,2560]{1,0:T(8,128)(2,1)S(1)}, u32[]{:S(2)}, u32[]{:S(2)}) collective-permute-start(bf16[128,2560]{1,0:T(8,128)(2,1)} %get-tuple-element.29), channel_id=1, source_target_pairs={{0,1},{1,0},{2,3},{3,2},{4,5},{5,4},{6,7},{7,6},{8,9},{9,8},{10,11... | collective-permute-start | bytes 1966088 | tf_op jit(solution)/shard_map/ppermute | solution.py:219
  19.4 1.9 %collective-permute-start.1 = (bf16[128,1280]{1,0:T(8,128)(2,1)}, bf16[128,1280]{1,0:T(8,128)(2,1)S(1)}, u32[]{:S(2)}, u32[]{:S(2)}) collective-permute-start(bf16[128,1280]{1,0:T(8,128)(2,1)} %get-tuple-element.30), channel_id=1, source_target_pairs={{0,2},{1,3},{2,0},{3,1},{4,6},{5,7},{6,4},{7,5},{8,10},{9,11},{10,... | collective-permute-start | bytes 983048 | tf_op jit(solution)/shard_map/ppermute | solution.py:219
  21.3 3.5 %collective-permute-start.2 = (bf16[128,1280]{1,0:T(8,128)(2,1)}, bf16[128,1280]{1,0:T(8,128)(2,1)S(1)}, u32[]{:S(2)}, u32[]{:S(2)}) collective-permute-start(bf16[128,1280]{1,0:T(8,128)(2,1)} %get-tuple-element.31), channel_id=1, source_target_pairs={{0,3},{1,2},{2,1},{3,0},{4,7},{5,6},{6,5},{7,4},{8,11},{9,10},{10,... | collective-permute-start | bytes 983048 | tf_op jit(solution)/shard_map/ppermute | solution.py:219
  24.8 3.4 %shard_map.110 = (bf16[128,1280]{1,0:T(8,128)(2,1)}, bf16[128,1280]{1,0:T(8,128)(2,1)}, bf16[128,2560]{1,0:T(8,128)(2,1)}, bf16[256,256]{1,0:T(8,128)(2,1)}) custom-call(s32[4]{0:T(128)} %frag.3, bf16[128,8192]{1,0:T(8,128)(2,1)} %bitcast.16, bf16[128,512]{1,0:T(8,128)(2,1)} %bitcast.18, bf16[256,512]{1,0:T(8,128)(2,1)} %bitcast.10), custom_call_target="tpu_custom_call" | custom-call | tf_op jit(solution)/shard_map/pallas_call | solution.py:198
  28.2 1.9 %collective-permute-start.3 = (bf16[128,1280]{1,0:T(8,128)(2,1)}, bf16[128,1280]{1,0:T(8,128)(2,1)S(1)}, u32[]{:S(2)}, u32[]{:S(2)}) collective-permute-start(bf16[128,1280]{1,0:T(8,128)(2,1)} %get-tuple-element.32), channel_id=1, source_target_pairs={{0,2},{1,3},{2,0},{3,1},{4,6},{5,7},{6,4},{7,5},{8,10},{9,11},{10,... | collective-permute-start | bytes 983048 | tf_op jit(solution)/shard_map/ppermute | solution.py:219
  30.2 3.7 %collective-permute-start.4 = (bf16[128,1280]{1,0:T(8,128)(2,1)}, bf16[128,1280]{1,0:T(8,128)(2,1)S(1)}, u32[]{:S(2)}, u32[]{:S(2)}) collective-permute-start(bf16[128,1280]{1,0:T(8,128)(2,1)} %get-tuple-element.33), channel_id=1, source_target_pairs={{0,3},{1,2},{2,1},{3,0},{4,7},{5,6},{6,5},{7,4},{8,11},{9,10},{10,... | collective-permute-start | bytes 983048 | tf_op jit(solution)/shard_map/ppermute | solution.py:219
  33.9 4.0 %all-to-all-start = ((bf16[16,16,256]{2,1,0:T(8,128)(2,1)}), bf16[16,16,256]{2,1,0:T(8,128)(2,1)S(1)}, u32[]{:S(2)}, u32[]{:S(2)}) async-start(bf16[16,16,256]{2,1,0:T(8,128)(2,1)} %bitcast.20), calls=%async_computation | async-start | bytes 262144 | tf_op jit(solution)/shard_map/all_to_all | solution.py:235
  41.3 10.0 %collective-permute-start.8 = (s16[272,512]{1,0:T(8,128)(2,1)}, s16[272,512]{1,0:T(8,128)(2,1)}, u32[]{:S(2)}, u32[]{:S(2)}) collective-permute-start(s16[272,512]{1,0:T(8,128)(2,1)} %get-tuple-element.39), channel_id=1, source_target_pairs={{0,8},{1,25},{2,10},{3,27},{4,12},{5,29},{6,14},{7,31},{8,16},{9,1... | collective-permute-start | bytes 835592 | tf_op jit(solution)/shard_map/ppermute | solution.py:219
  51.3 2.2 %collective-permute-start.9 = (s16[272,512]{1,0:T(8,128)(2,1)}, s16[272,512]{1,0:T(8,128)(2,1)}, u32[]{:S(2)}, u32[]{:S(2)}) collective-permute-start(s16[272,512]{1,0:T(8,128)(2,1)} %get-tuple-element.40), channel_id=1, source_target_pairs={{0,4},{1,29},{2,6},{3,31},{4,8},{5,1},{6,10},{7,3},{8,12},{9,5},{1... | collective-permute-start | bytes 835592 | tf_op jit(solution)/shard_map/ppermute | solution.py:219
  53.5 3.1 %collective-permute-start.10 = (s16[272,512]{1,0:T(8,128)(2,1)}, s16[272,512]{1,0:T(8,128)(2,1)}, u32[]{:S(2)}, u32[]{:S(2)}) collective-permute-start(s16[272,512]{1,0:T(8,128)(2,1)} %get-tuple-element.41), channel_id=1, source_target_pairs={{0,28},{1,5},{2,30},{3,7},{4,0},{5,9},{6,2},{7,11},{8,4},{9,13},{1... | collective-permute-start | bytes 835592 | tf_op jit(solution)/shard_map/ppermute | solution.py:219
  58.7 3.4 %collective-permute-start.13 = (s16[272,512]{1,0:T(8,128)(2,1)}, s16[272,512]{1,0:T(8,128)(2,1)S(1)}, u32[]{:S(2)}, u32[]{:S(2)}) collective-permute-start(s16[272,512]{1,0:T(8,128)(2,1)} %get-tuple-element.44), channel_id=1, source_target_pairs={{0,4},{1,29},{2,6},{3,31},{4,8},{5,1},{6,10},{7,3},{8,12},{9,5},{1... | collective-permute-start | bytes 835592 | tf_op jit(solution)/shard_map/ppermute | solution.py:219
  62.1 1.9 %collective-permute-start.14 = (s16[272,512]{1,0:T(8,128)(2,1)}, s16[272,512]{1,0:T(8,128)(2,1)}, u32[]{:S(2)}, u32[]{:S(2)}) collective-permute-start(s16[272,512]{1,0:T(8,128)(2,1)} %get-tuple-element.45), channel_id=1, source_target_pairs={{0,28},{1,5},{2,30},{3,7},{4,0},{5,9},{6,2},{7,11},{8,4},{9,13},{1... | collective-permute-start | bytes 835592 | tf_op jit(solution)/shard_map/ppermute | solution.py:219
  64.8 9.1 %all-to-all-start.1 = ((f32[16,16,256]{2,1,0:T(8,128)}), f32[16,16,256]{2,1,0:T(8,128)S(1)}, u32[]{:S(2)}, u32[]{:S(2)}) async-start(f32[16,16,256]{2,1,0:T(8,128)} %broadcast_in_dim.16), calls=%async_computation.1 | async-start | bytes 524288 | tf_op jit(solution)/shard_map/all_to_all | solution.py:248
  73.9 2.4 %shard_map.116 = (s16[272,512]{1,0:T(8,128)(2,1)}, s16[272,512]{1,0:T(8,128)(2,1)}) custom-call(bf16[128,2560]{1,0:T(8,128)(2,1)S(1)} %copy-done.1, bf16[128,2560]{1,0:T(8,128)(2,1)S(1)} %collective-permute-done.near, bf16[128,1280]{1,0:T(8,128)(2,1)S(1)} %collective-permute-done.1.y_early, bf16[128,1280]{1,0:T(8,128)(2,1)S(1)} %collective-permute-done.2.x_early, ...), custom_call_target="tpu_custom_call" | custom-call | tf_op jit(solution)/shard_map/pallas_call | solution.py:198
  76.3 3.1 %collective-permute-start.11 = (s16[272,512]{1,0:T(8,128)(2,1)}, s16[272,512]{1,0:T(8,128)(2,1)}, u32[]{:S(2)}, u32[]{:S(2)}) collective-permute-start(s16[272,512]{1,0:T(8,128)(2,1)} %get-tuple-element.42), channel_id=1, source_target_pairs={{0,8},{1,25},{2,10},{3,27},{4,12},{5,29},{6,14},{7,31},{8,16},{9,1... | collective-permute-start | bytes 835592 | tf_op jit(solution)/shard_map/ppermute | solution.py:219
  79.4 3.1 %collective-permute-start.12 = (s16[272,512]{1,0:T(8,128)(2,1)}, s16[272,512]{1,0:T(8,128)(2,1)}, u32[]{:S(2)}, u32[]{:S(2)}) collective-permute-start(s16[272,512]{1,0:T(8,128)(2,1)} %get-tuple-element.43), channel_id=1, source_target_pairs={{0,24},{1,9},{2,26},{3,11},{4,28},{5,13},{6,30},{7,15},{8,0},{9,17... | collective-permute-start | bytes 835592 | tf_op jit(solution)/shard_map/ppermute | solution.py:219
  82.6 1.6 %copy-done.3 = bf16[1,2048,512]{2,1,0:T(8,128)(2,1)S(1)} copy-done((bf16[1,2048,512]{2,1,0:T(8,128)(2,1)S(1)}, bf16[1,2048,512]{2,1,0:T(8,128)(2,1)}, u32[]{:S(2)}) %copy-start.3) | copy-done | bytes 2097176
  84.2 2.0 %shard_map.112 = (f32[128,512]{1,0:T(8,128)S(1)}, f32[128,512]{1,0:T(8,128)}, f32[128,512]{1,0:T(8,128)}, f32[128,512]{1,0:T(8,128)}) custom-call(bf16[128,2560]{1,0:T(8,128)(2,1)S(1)} %copy-done.1, bf16[128,2560]{1,0:T(8,128)(2,1)S(1)} %collective-permute-done.near, bf16[128,1280]{1,0:T(8,128)(2,1)S(1)} %collective-permute-done.1.y_early, ...), custom_call_target="tpu_custom_call" | custom-call | tf_op jit(solution)/shard_map/pallas_call | solution.py:198
  86.8 5.1 %collective-permute-start.5 = (f32[128,512]{1,0:T(8,128)}, f32[128,512]{1,0:T(8,128)S(1)}, u32[]{:S(2)}, u32[]{:S(2)}) collective-permute-start(f32[128,512]{1,0:T(8,128)} %get-tuple-element.35), channel_id=1, source_target_pairs={{0,1},{1,0},{2,3},{3,2},{4,5},{5,4},{6,7},{7,6},{8,9},{9,8},{10,11... | collective-permute-start | bytes 786440 | tf_op jit(solution)/shard_map/ppermute | solution.py:219
  92.0 2.3 %collective-permute-start.6 = (f32[128,512]{1,0:T(8,128)}, f32[128,512]{1,0:T(8,128)S(1)}, u32[]{:S(2)}, u32[]{:S(2)}) collective-permute-start(f32[128,512]{1,0:T(8,128)} %get-tuple-element.36), channel_id=1, source_target_pairs={{0,2},{1,3},{2,0},{3,1},{4,6},{5,7},{6,4},{7,5},{8,10},{9,11},{10,... | collective-permute-start | bytes 786440 | tf_op jit(solution)/shard_map/ppermute | solution.py:219
  94.3 3.2 %collective-permute-start.7 = (f32[128,512]{1,0:T(8,128)}, f32[128,512]{1,0:T(8,128)S(1)}, u32[]{:S(2)}, u32[]{:S(2)}) collective-permute-start(f32[128,512]{1,0:T(8,128)} %get-tuple-element.37), channel_id=1, source_target_pairs={{0,3},{1,2},{2,1},{3,0},{4,7},{5,6},{6,5},{7,4},{8,11},{9,10},{10,... | collective-permute-start | bytes 786440 | tf_op jit(solution)/shard_map/ppermute | solution.py:219
  101.5 3.0 %shard_map.117 = (f32[256,512]{1,0:T(8,128)}, bf16[256,512]{1,0:T(8,128)(2,1)}, f32[2,256,128]{2,1,0:T(8,128)}, f32[2,256,128]{2,1,0:T(8,128)}) custom-call(s32[4]{0:T(128)S(1)} %copy-done.11, f32[256,512]{1,0:T(8,128)S(1)} %copy-done.6, s16[272,512]{1,0:T(8,128)(2,1)} %collective-permute-done.11.ahead2, s16[272,512]{1,0:T(8,128)(2,1)} %collective-permute-done.12.behind2, ...), custom_call_target="tpu_custom_call" | custom-call | tf_op jit(solution)/shard_map/pallas_call | solution.py:198
  104.5 3.2 %collective-permute-done.7.d = f32[128,512]{1,0:T(8,128)S(1)} collective-permute-done((f32[128,512]{1,0:T(8,128)}, f32[128,512]{1,0:T(8,128)S(1)}, u32[]{:S(2)}, u32[]{:S(2)}) %collective-permute-start.7) | collective-permute-done | bytes 262176 | tf_op jit(solution)/shard_map/ppermute | solution.py:219
  (47 shorter events, 12.4 us)
Async XLA Ops:
  7.2 75.4 %all-gather.3.cloned.1.call-start = ((), (), s32[]{:S(2)}) async-start(), calls=%async_computation.2 | async-start | bytes 2359296 | tf_op jit(solution)/shard_map/all_gather | solution.py:217
  10.6 28.2 %collective-permute-start = (bf16[128,2560]{1,0:T(8,128)(2,1)}, bf16[128,2560]{1,0:T(8,128)(2,1)S(1)}, u32[]{:S(2)}, u32[]{:S(2)}) collective-permute-start(bf16[128,2560]{1,0:T(8,128)(2,1)} %get-tuple-element.29), channel_id=1, source_target_pairs={{0,1},{1,0},{2,3},{3,2},{4,5},{5,4},{6,7},{7,6},{8,9},{9,8},{10,11... | collective-permute-start | bytes 1966088 | tf_op jit(solution)/shard_map/ppermute | solution.py:219
  19.4 18.6 %collective-permute-start.1 = (bf16[128,1280]{1,0:T(8,128)(2,1)}, bf16[128,1280]{1,0:T(8,128)(2,1)S(1)}, u32[]{:S(2)}, u32[]{:S(2)}) collective-permute-start(bf16[128,1280]{1,0:T(8,128)(2,1)} %get-tuple-element.30), channel_id=1, source_target_pairs={{0,2},{1,3},{2,0},{3,1},{4,6},{5,7},{6,4},{7,5},{8,10},{9,11},{10,... | collective-permute-start | bytes 983048 | tf_op jit(solution)/shard_map/ppermute | solution.py:219
  21.3 17.4 %collective-permute-start.2 = (bf16[128,1280]{1,0:T(8,128)(2,1)}, bf16[128,1280]{1,0:T(8,128)(2,1)S(1)}, u32[]{:S(2)}, u32[]{:S(2)}) collective-permute-start(bf16[128,1280]{1,0:T(8,128)(2,1)} %get-tuple-element.31), channel_id=1, source_target_pairs={{0,3},{1,2},{2,1},{3,0},{4,7},{5,6},{6,5},{7,4},{8,11},{9,10},{10,... | collective-permute-start | bytes 983048 | tf_op jit(solution)/shard_map/ppermute | solution.py:219
  28.2 28.4 %collective-permute-start.3 = (bf16[128,1280]{1,0:T(8,128)(2,1)}, bf16[128,1280]{1,0:T(8,128)(2,1)S(1)}, u32[]{:S(2)}, u32[]{:S(2)}) collective-permute-start(bf16[128,1280]{1,0:T(8,128)(2,1)} %get-tuple-element.32), channel_id=1, source_target_pairs={{0,2},{1,3},{2,0},{3,1},{4,6},{5,7},{6,4},{7,5},{8,10},{9,11},{10,... | collective-permute-start | bytes 983048 | tf_op jit(solution)/shard_map/ppermute | solution.py:219
  30.2 26.5 %collective-permute-start.4 = (bf16[128,1280]{1,0:T(8,128)(2,1)}, bf16[128,1280]{1,0:T(8,128)(2,1)S(1)}, u32[]{:S(2)}, u32[]{:S(2)}) collective-permute-start(bf16[128,1280]{1,0:T(8,128)(2,1)} %get-tuple-element.33), channel_id=1, source_target_pairs={{0,3},{1,2},{2,1},{3,0},{4,7},{5,6},{6,5},{7,4},{8,11},{9,10},{10,... | collective-permute-start | bytes 983048 | tf_op jit(solution)/shard_map/ppermute | solution.py:219
  33.9 30.2 %all-to-all-start = ((bf16[16,16,256]{2,1,0:T(8,128)(2,1)}), bf16[16,16,256]{2,1,0:T(8,128)(2,1)S(1)}, u32[]{:S(2)}, u32[]{:S(2)}) async-start(bf16[16,16,256]{2,1,0:T(8,128)(2,1)} %bitcast.20), calls=%async_computation | async-start | bytes 262144 | tf_op jit(solution)/shard_map/all_to_all | solution.py:235
  38.7 1.1 copy-start
  41.3 32.6 %copy-start.1 = (bf16[128,2560]{1,0:T(8,128)(2,1)S(1)}, bf16[128,2560]{1,0:T(8,128)(2,1)}, u32[]{:S(2)}) copy-start(bf16[128,2560]{1,0:T(8,128)(2,1)} %get-tuple-element.28.own) | copy-start | bytes 1966084
  41.3 32.6 %collective-permute-start.8 = (s16[272,512]{1,0:T(8,128)(2,1)}, s16[272,512]{1,0:T(8,128)(2,1)}, u32[]{:S(2)}, u32[]{:S(2)}) collective-permute-start(s16[272,512]{1,0:T(8,128)(2,1)} %get-tuple-element.39), channel_id=1, source_target_pairs={{0,8},{1,25},{2,10},{3,27},{4,12},{5,29},{6,14},{7,31},{8,16},{9,1... | collective-permute-start | bytes 835592 | tf_op jit(solution)/shard_map/ppermute | solution.py:219
  51.3 22.6 %collective-permute-start.9 = (s16[272,512]{1,0:T(8,128)(2,1)}, s16[272,512]{1,0:T(8,128)(2,1)}, u32[]{:S(2)}, u32[]{:S(2)}) collective-permute-start(s16[272,512]{1,0:T(8,128)(2,1)} %get-tuple-element.40), channel_id=1, source_target_pairs={{0,4},{1,29},{2,6},{3,31},{4,8},{5,1},{6,10},{7,3},{8,12},{9,5},{1... | collective-permute-start | bytes 835592 | tf_op jit(solution)/shard_map/ppermute | solution.py:219
  53.5 20.4 %collective-permute-start.10 = (s16[272,512]{1,0:T(8,128)(2,1)}, s16[272,512]{1,0:T(8,128)(2,1)}, u32[]{:S(2)}, u32[]{:S(2)}) collective-permute-start(s16[272,512]{1,0:T(8,128)(2,1)} %get-tuple-element.41), channel_id=1, source_target_pairs={{0,28},{1,5},{2,30},{3,7},{4,0},{5,9},{6,2},{7,11},{8,4},{9,13},{1... | collective-permute-start | bytes 835592 | tf_op jit(solution)/shard_map/ppermute | solution.py:219
  58.7 33.2 %collective-permute-start.13 = (s16[272,512]{1,0:T(8,128)(2,1)}, s16[272,512]{1,0:T(8,128)(2,1)S(1)}, u32[]{:S(2)}, u32[]{:S(2)}) collective-permute-start(s16[272,512]{1,0:T(8,128)(2,1)} %get-tuple-element.44), channel_id=1, source_target_pairs={{0,4},{1,29},{2,6},{3,31},{4,8},{5,1},{6,10},{7,3},{8,12},{9,5},{1... | collective-permute-start | bytes 835592 | tf_op jit(solution)/shard_map/ppermute | solution.py:219
  62.1 32.1 %collective-permute-start.14 = (s16[272,512]{1,0:T(8,128)(2,1)}, s16[272,512]{1,0:T(8,128)(2,1)}, u32[]{:S(2)}, u32[]{:S(2)}) collective-permute-start(s16[272,512]{1,0:T(8,128)(2,1)} %get-tuple-element.45), channel_id=1, source_target_pairs={{0,28},{1,5},{2,30},{3,7},{4,0},{5,9},{6,2},{7,11},{8,4},{9,13},{1... | collective-permute-start | bytes 835592 | tf_op jit(solution)/shard_map/ppermute | solution.py:219
  64.8 32.6 %all-to-all-start.1 = ((f32[16,16,256]{2,1,0:T(8,128)}), f32[16,16,256]{2,1,0:T(8,128)S(1)}, u32[]{:S(2)}, u32[]{:S(2)}) async-start(f32[16,16,256]{2,1,0:T(8,128)} %broadcast_in_dim.16), calls=%async_computation.1 | async-start | bytes 524288 | tf_op jit(solution)/shard_map/all_to_all | solution.py:248
  76.3 21.1 %collective-permute-start.11 = (s16[272,512]{1,0:T(8,128)(2,1)}, s16[272,512]{1,0:T(8,128)(2,1)}, u32[]{:S(2)}, u32[]{:S(2)}) collective-permute-start(s16[272,512]{1,0:T(8,128)(2,1)} %get-tuple-element.42), channel_id=1, source_target_pairs={{0,8},{1,25},{2,10},{3,27},{4,12},{5,29},{6,14},{7,31},{8,16},{9,1... | collective-permute-start | bytes 835592 | tf_op jit(solution)/shard_map/ppermute | solution.py:219
  79.4 18.0 %collective-permute-start.12 = (s16[272,512]{1,0:T(8,128)(2,1)}, s16[272,512]{1,0:T(8,128)(2,1)}, u32[]{:S(2)}, u32[]{:S(2)}) collective-permute-start(s16[272,512]{1,0:T(8,128)(2,1)} %get-tuple-element.43), channel_id=1, source_target_pairs={{0,24},{1,9},{2,26},{3,11},{4,28},{5,13},{6,30},{7,15},{8,0},{9,17... | collective-permute-start | bytes 835592 | tf_op jit(solution)/shard_map/ppermute | solution.py:219
  82.6 1.6 %copy-start.3 = (bf16[1,2048,512]{2,1,0:T(8,128)(2,1)S(1)}, bf16[1,2048,512]{2,1,0:T(8,128)(2,1)}, u32[]{:S(2)}) copy-start(bf16[1,2048,512]{2,1,0:T(8,128)(2,1)} %all-gather.3.cloned.1.call-done) | copy-start | bytes 6291460
  84.2 13.3 %copy-start.2 = (bf16[1,256,512]{2,1,0:T(8,128)(2,1)S(1)}, bf16[1,256,512]{2,1,0:T(8,128)(2,1)}, u32[]{:S(2)}) copy-start(bf16[1,256,512]{2,1,0:T(8,128)(2,1)} %param.9) | copy-start | bytes 786436
  84.2 13.3 %copy-start.11 = (s32[4]{0:T(128)S(1)}, s32[4]{0:T(128)}, u32[]{:S(2)}) copy-start(s32[4]{0:T(128)} %frag.3) | copy-start | bytes 52
  86.8 17.7 %collective-permute-start.5 = (f32[128,512]{1,0:T(8,128)}, f32[128,512]{1,0:T(8,128)S(1)}, u32[]{:S(2)}, u32[]{:S(2)}) collective-permute-start(f32[128,512]{1,0:T(8,128)} %get-tuple-element.35), channel_id=1, source_target_pairs={{0,1},{1,0},{2,3},{3,2},{4,5},{5,4},{6,7},{7,6},{8,9},{9,8},{10,11... | collective-permute-start | bytes 786440 | tf_op jit(solution)/shard_map/ppermute | solution.py:219
  92.0 12.6 %collective-permute-start.6 = (f32[128,512]{1,0:T(8,128)}, f32[128,512]{1,0:T(8,128)S(1)}, u32[]{:S(2)}, u32[]{:S(2)}) collective-permute-start(f32[128,512]{1,0:T(8,128)} %get-tuple-element.36), channel_id=1, source_target_pairs={{0,2},{1,3},{2,0},{3,1},{4,6},{5,7},{6,4},{7,5},{8,10},{9,11},{10,... | collective-permute-start | bytes 786440 | tf_op jit(solution)/shard_map/ppermute | solution.py:219
  94.3 13.4 %collective-permute-start.7 = (f32[128,512]{1,0:T(8,128)}, f32[128,512]{1,0:T(8,128)S(1)}, u32[]{:S(2)}, u32[]{:S(2)}) collective-permute-start(f32[128,512]{1,0:T(8,128)} %get-tuple-element.37), channel_id=1, source_target_pairs={{0,3},{1,2},{2,1},{3,0},{4,7},{5,6},{6,5},{7,4},{8,11},{9,10},{10,... | collective-permute-start | bytes 786440 | tf_op jit(solution)/shard_map/ppermute | solution.py:219
  101.5 6.2 %copy-start.8 = (f32[128,512]{1,0:T(8,128)S(1)}, f32[128,512]{1,0:T(8,128)}, u32[]{:S(2)}) copy-start(f32[128,512]{1,0:T(8,128)} %copy-done.7) | copy-start | bytes 786436
  (6 other events, 5.5 us)
Sparse Core Ops, SparseCore 0:
  10.1 50.8 all-gather.2

commit v2 on v1

v2 whole, which is shorter than its diff:
```python
import functools

import jax
import jax.numpy as jnp
from jax import lax
from jax.experimental import pallas as pl
from jax.experimental.pallas import tpu as pltpu
from jax.sharding import PartitionSpec as P

D = 8192
HD = 128
KVH = 4

LR_INNER = 0.1
BETA_INNER = 0.9
MU_OUTER = 0.9
LR_OUTER = 0.7
ALPHA_MIX = 0.5

F32 = jnp.float32
BF16 = jnp.bfloat16

NZ, NY, NC = 8, 2, 2
NX, NR = 4, 4
NG = NY * NC

ROWS = 256
TOK = 128
EARLY = (4, 3, 1, -3, -1)
LATE = (2, -2, 0)
DIST = EARLY + LATE
SPLIT = len(EARLY) * ROWS + KVH * HD
WIDE = SPLIT + len(LATE) * ROWS
LEVELS = 32000.0
CODED = ROWS + 16


def place(z, y, c):
    return ((z % NZ) * NY + y) * NC + c


def ring(dist):
    return [
        (place(z, y, c), place(z + (dist if c == 0 else -dist), y, c))
        for z in range(NZ) for y in range(NY) for c in range(NC)
    ]


def swap(k):
    return [(f, f ^ k) for f in range(NZ * NG)]


def z_groups():
    return [[place(z, y, c) for z in range(NZ)] for y in range(NY) for c in range(NC)]


def x_groups():
    return [[x * NR + y for x in range(NX)] for y in range(NR)]


def y_groups():
    return [[x * NR + y for y in range(NR)] for x in range(NX)]


def owner(dist, k=0):
    me = lax.axis_index("fsdp")
    z = me // NG
    forward = 1 - 2 * ((me % NC) ^ (k % NC))
    return (z + forward * dist + NZ) % NZ


def column_of(i):
    first = 0 if i < len(EARLY) else KVH * HD
    return first + i * ROWS


def piece_of(tok, i, k):
    me = lax.axis_index("fsdp")
    block = owner(DIST[i], k) * NG + ((me % NG) ^ k)
    return tok.at[:, pl.ds(pl.multiple_of(block * ROWS, ROWS), ROWS)]


def copy_all(pairs, sems):
    copies = [pltpu.make_async_copy(src, dst, sems.at[n]) for n, (src, dst) in enumerate(pairs)]
    for copy in copies:
        copy.start()
    for copy in copies:
        copy.wait()


def pack_early_kernel(tok, cot, y_early, x_early, near, sems):
    pairs = []
    for out, k in ((y_early, 2), (x_early, 3), (near, 1)):
        for i in range(len(DIST) if k == 1 else len(EARLY)):
            pairs.append((piece_of(tok, i, k), out.at[:, pl.ds(column_of(i), ROWS)]))
        pairs.append((cot, out.at[:, pl.ds(SPLIT - KVH * HD, KVH * HD)]))
    copy_all(pairs, sems)


def pack_late_kernel(frag, tok, cot, w, y_late, x_late, own, picked, sems):
    pairs = []
    for out, k in ((y_late, 2), (x_late, 3)):
        for i in range(len(EARLY), len(DIST)):
            pairs.append((piece_of(tok, i, k), out.at[:, pl.ds(column_of(i) - SPLIT, ROWS)]))
    for i in range(len(DIST)):
        pairs.append((piece_of(tok, i, 0), own.at[:, pl.ds(column_of(i), ROWS)]))
    pairs.append((cot, own.at[:, pl.ds(SPLIT - KVH * HD, KVH * HD)]))
    for k in range(2):
        src = w.at[:, pl.ds(pl.multiple_of(frag[k] * HD, HD), HD)]
        pairs += [(src, picked.at[n, :, pl.ds(k * HD, HD)]) for n in range(NX)]
    copy_all(pairs, sems)


def encode(x, out, at=0):
    top = jnp.max(jnp.abs(x), axis=0, keepdims=True)
    power = jnp.ceil(jnp.log2(jnp.maximum(top, 1e-30)))
    out[at : at + ROWS, :] = jnp.round(x * (LEVELS * jnp.exp2(-power))).astype(jnp.int32).astype(jnp.int16)
    out[at + ROWS : at + CODED, :] = (
        jnp.broadcast_to(power, (CODED - ROWS, x.shape[1])).astype(jnp.int32).astype(jnp.int16)
    )


def decode(ref, at=0):
    power = ref[at + ROWS : at + CODED, :].astype(jnp.int32).astype(F32)[0:1]
    return ref[at : at + ROWS, :].astype(jnp.int32).astype(F32) * (jnp.exp2(power) * (1.0 / LEVELS))


def partial_grad(refs, cot, dist):
    columns = [block_of(first, second, DIST.index(dist)) for first, second in refs]
    features = jnp.concatenate(columns, axis=0)
    return lax.dot_general(features, cot, (((0,), (0,)), ((), ())), preferred_element_type=F32)


def block_of(first, second, i):
    at = column_of(i)
    if second is None or at < SPLIT:
        return first[:, at : at + ROWS]
    return second[:, at - SPLIT : at - SPLIT + ROWS]


def cotangents(refs):
    return jnp.concatenate([r[:, SPLIT - KVH * HD : SPLIT] for r, _ in refs], axis=0)


def early_kernel(own, near, y_early, x_early, far, ahead, behind):
    refs = [(r, None) for r in (own, near, y_early, x_early)]
    cot = cotangents(refs)
    encode(partial_grad(refs, cot, 4), far)
    encode(partial_grad(refs, cot, 3), ahead)
    encode(partial_grad(refs, cot, 1), ahead, CODED)
    encode(partial_grad(refs, cot, -3), behind)
    encode(partial_grad(refs, cot, -1), behind, CODED)


def late_kernel(own, near, y_early, x_early, y_late, x_late, ahead2, behind2):
    refs = [(own, None), (near, None), (y_early, y_late), (x_early, x_late)]
    cot = cotangents(refs)
    ahead2[...] = partial_grad(refs, cot, 2)
    behind2[...] = partial_grad(refs, cot, -2)


def relay_kernel(mine_ahead, mine_behind, far, ahead, behind, ahead2, behind2):
    encode(mine_ahead[...] + decode(far) + decode(ahead), ahead2)
    encode(mine_behind[...] + decode(behind), behind2)


def key_kernel(own, near, y_early, x_early, y_late, x_late, w, moment, base, kept, sent):
    refs = [(own, None), (near, None), (y_early, y_late), (x_early, x_late)]
    for out, at, (first, second) in zip((kept, sent, kept, sent), (0, 0, TOK, TOK), refs):
        total = jnp.zeros((TOK, KVH * HD), F32)
        for i, dist in enumerate(DIST):
            rows = w[pl.ds(pl.multiple_of(owner(dist) * ROWS, ROWS), ROWS), :]
            total = total + jnp.dot(block_of(first, second, i), rows, preferred_element_type=F32)
        out[at : at + TOK, :] = total
    base[...] = BETA_INNER * moment[...] + partial_grad(refs, cotangents(refs), 0) * (D ** -0.5)


def picked_sum_kernel(picked, out):
    total = picked[0].astype(F32)
    for n in range(1, NX):
        total = total + picked[n].astype(F32)
    encode(total, out.at[0])
    for n in range(1, NR):
        out[n] = out[0]


def outer_kernel(sums, gf, om, global_new, outer_new, blend, *, replicas):
    total = decode(sums.at[0])
    for n in range(1, NR):
        total = total + decode(sums.at[n])
    for k in range(2):
        mean = gf[k] - total[:, k * HD : (k + 1) * HD] * (1.0 / replicas)
        out = MU_OUTER * om[k] + mean
        outer_new[k] = out
        new = gf[k] - LR_OUTER * (MU_OUTER * out + mean)
        global_new[k] = new
        blend[k] = (1.0 - ALPHA_MIX) * new


def update_kernel(frag, base, ahead2, behind2, ahead, behind, w, blend, moment_new, weight_new):
    others = decode(ahead2) + decode(behind2) + decode(ahead, CODED) + decode(behind, CODED)
    new = base[...] + others * (D ** -0.5)
    moment_new[...] = new
    inner = w[...].astype(F32) - LR_INNER * new
    for h in range(KVH):
        mine = inner[:, h * HD : (h + 1) * HD]
        first = ALPHA_MIX * mine + blend[0]
        second = ALPHA_MIX * mine + blend[1]
        merged = jnp.where(frag[0] == h, first, jnp.where(frag[1] == h, second, mine))
        weight_new[:, h * HD : (h + 1) * HD] = merged.astype(BF16)


def key_half_kernel(kept, got, mine, theirs):
    mine[...] = kept[:TOK, :] + got[:TOK, :]
    theirs[...] = kept[TOK:, :] + got[TOK:, :]


def key_sum_kernel(mine, got, out):
    out[...] = ((mine[...] + got[...]) * (D ** -0.5)).astype(BF16)


def call(kernel, outs, *args, scalars=0, copies=0, hint=0, first=False):
    space = pl.ANY if copies else pltpu.VMEM
    specs = [pl.BlockSpec(memory_space=pltpu.SMEM)] * scalars
    specs += [pl.BlockSpec(memory_space=space)] * (len(args) - scalars)
    return pl.pallas_call(
        kernel,
        out_shape=list(outs),
        in_specs=specs,
        out_specs=[pl.BlockSpec(memory_space=pltpu.VMEM)] * len(outs),
        scratch_shapes=[pltpu.SemaphoreType.DMA((copies,))] if copies else [],
        compiler_params=None if first else pltpu.CompilerParams(vmem_limit_bytes=16 * 2**20),
        cost_estimate=pl.CostEstimate(flops=hint * 10**9, bytes_accessed=0, transcendentals=0),
    )(*args)


def shape(*dims, kind=BF16):
    return jax.ShapeDtypeStruct(dims, kind)


def shards(tokens, cotangent, weight, moment, global_frag, outer_moment, fragment):
    replicas = lax.axis_size("rep")
    width = KVH * HD
    w = weight[0]
    w_rows = lax.all_gather(w, "fsdp", axis_index_groups=z_groups(), tiled=True)

    send = lambda x, pairs: lax.ppermute(x, "fsdp", pairs)
    y_early, x_early, near = call(
        pack_early_kernel, [shape(TOK, SPLIT)] * 2 + [shape(TOK, WIDE)], tokens[0], cotangent[0],
        copies=2 * len(EARLY) + len(DIST) + 3, first=True,
    )
    y_early = send(y_early, swap(2))
    x_early = send(x_early, swap(3))
    near = send(near, swap(1))
    y_late, x_late, own, picked = call(
        pack_late_kernel,
        [shape(TOK, WIDE - SPLIT)] * 2 + [shape(TOK, WIDE), shape(NX, ROWS, 2 * HD)],
        fragment, tokens[0], cotangent[0], w, scalars=1, copies=2 * len(LATE) + len(DIST) + 1 + 2 * NX,
    )
    y_late = send(y_late, swap(2))
    x_late = send(x_late, swap(3))

    picked = lax.all_to_all(picked, "rep", 0, 0, axis_index_groups=x_groups())

    one = shape(CODED, width, kind=jnp.int16)
    two = shape(2 * CODED, width, kind=jnp.int16)
    wide = shape(ROWS, width, kind=F32)
    far, ahead, behind = call(early_kernel, [one, two, two], own, near, y_early, x_early)
    far, y_late = lax.optimization_barrier((far, y_late))
    far = send(far, ring(2))
    ahead = send(ahead, ring(1))
    behind = send(behind, ring(-1))
    got = (own, near, y_early, x_early, y_late, x_late)
    mine = call(late_kernel, [wide] * 2, *got, hint=14)
    (sums,) = call(picked_sum_kernel, [shape(NR, CODED, 2 * HD, kind=jnp.int16)], picked)
    sums = lax.all_to_all(sums, "rep", 0, 0, axis_index_groups=y_groups())
    outer = shape(2, ROWS, HD, kind=F32)
    global_new, outer_new, blend = call(
        functools.partial(outer_kernel, replicas=replicas), [outer] * 3, sums, global_frag, outer_moment
    )
    pair = shape(2 * TOK, width, kind=F32)
    base, kept, sent = call(key_kernel, [wide, pair, pair], *got, w_rows, moment[0])
    half = shape(TOK, width, kind=F32)
    mine_key, theirs_key = call(key_half_kernel, [half] * 2, kept, send(sent, swap(1)))
    base, far = lax.optimization_barrier((base, far))
    ahead2, behind2 = call(relay_kernel, [one] * 2, *mine, far, ahead, behind)
    ahead2 = send(ahead2, ring(2))
    behind2 = send(behind2, ring(-2))
    (key_out,) = call(key_sum_kernel, [shape(TOK, width)], mine_key, send(theirs_key, swap(2)))

    moment_new, weight_new = call(
        update_kernel, [wide, shape(ROWS, width)],
        fragment, base, ahead2, behind2, ahead, behind, w, blend, scalars=1,
    )
    return key_out[None], moment_new[None], weight_new[None], global_new, outer_new


def solution(mesh):
    in_specs = (
        P("rep", "fsdp", None),
        P("rep", "fsdp", None),
        P("rep", "fsdp", None),
        P("rep", "fsdp", None),
        P(None, "fsdp", None),
        P(None, "fsdp", None),
        P(),
    )
    out_specs = (
        P("rep", "fsdp", None),
        P("rep", "fsdp", None),
        P("rep", "fsdp", None),
        P(None, "fsdp", None),
        P(None, "fsdp", None),
    )
    return jax.shard_map(shards, mesh=mesh, in_specs=in_specs, out_specs=out_specs, check_vma=False)
```

time: 116 us -> 112 us (0.966)
  starting transfers between devices: 70.4 us -> 51.9 us
  waiting for transfers between devices: 4.72 us -> 16.8 us
  Pallas kernels: 16.9 us -> 18.5 us
    ppermute x15 -> x12, starting transfers between devices: 57.3 us -> 44.9 us  [shards(): send = lambda x, pairs: lax.ppermute(x, 'fsdp', pairs)]
    ppermute x15 -> x12, waiting for transfers between devices: 4.01 us -> 12.4 us  [shards(): send = lambda x, pairs: lax.ppermute(x, 'fsdp', pairs)]
    all_to_all x2, starting transfers between devices: 13.1 us -> 6.94 us  [the longest x1 3.47 us: shards(): sums = lax.all_to_all(sums, 'rep', 0, 0, axis_index_groups=y_groups())]
    all_to_all x2, waiting for transfers between devices: 0.01 us -> 3.69 us  [the longest x1 3.69 us: shards(): picked = lax.all_to_all(picked, 'rep', 0, 0, axis_index_groups=x_groups())]
    pallas_call x8 -> x11, Pallas kernels: 16.9 us -> 18.5 us  [call(): pl.pallas_call(kernel, out_shape=list(outs), in_specs=specs, out_specs=[p...]
    unnamed x24 -> x32, local copies, waits for them, and re-layouts: 8.15 us -> 9.23 us
  transfers between devices with their start and end apart: 18 -> 15, of which waited for: 2 -> 4; matrix products, arithmetic and copies ran while one was open for 1% -> 0% of each run, Pallas kernels for 14% -> 16%
where the time goes in v2:
time: 112 us; the launch traced here: 111 us
  starting transfers between devices  51.9 us (46%)
  Pallas kernels  18.5 us (17%)
  waiting for transfers between devices  16.8 us (15%)
  between operations  14.3 us (13%)
  local copies, waits for them, and re-layouts  9.23 us (8%)
    ppermute x12, starting transfers between devices, shards(): send = lambda x, pairs: lax.ppermute(x, 'fsdp', pairs)  44.9 us
    pallas_call x11, Pallas kernels, call(): pl.pallas_call(kernel, out_shape=list(outs), in_specs=specs, out_specs=[p...  18.5 us
    ppermute x12, waiting for transfers between devices, shards(): send = lambda x, pairs: lax.ppermute(x, 'fsdp', pairs)  12.4 us
    unnamed x32, local copies, waits for them, and re-layouts  9.23 us
    all_to_all x1, waiting for transfers between devices, shards(): picked = lax.all_to_all(picked, 'rep', 0, 0, axis_index_groups=x_groups())  3.69 us
    all_to_all x1, starting transfers between devices, shards(): sums = lax.all_to_all(sums, 'rep', 0, 0, axis_index_groups=y_groups())  3.47 us
    all_to_all x1, starting transfers between devices, shards(): picked = lax.all_to_all(picked, 'rep', 0, 0, axis_index_groups=x_groups())  3.47 us
  transfers between devices with their start and end apart: 15, of which 4 were waited for; matrix products, arithmetic and copies ran while one was open for 0% of the time, Pallas kernels for 16%

profile of v2, /device:TPU:1, one launch (start us, length us, event | category | flops | bytes accessed | tf_op | source)
XLA Modules:
  0.0 110.8 jit_solution(15089606626333766369)
XLA Ops:
  7.9 2.8 %shard_map.111 = (bf16[128,1792]{1,0:T(8,128)(2,1)}, bf16[128,1792]{1,0:T(8,128)(2,1)}, bf16[128,2560]{1,0:T(8,128)(2,1)}) custom-call(bf16[128,8192]{1,0:T(8,128)(2,1)} %bitcast.8, bf16[128,512]{1,0:T(8,128)(2,1)} %bitcast.14), custom_call_target="tpu_custom_call" | custom-call | tf_op jit(solution)/shard_map/pallas_call | solution.py:226
  10.8 8.8 %collective-permute-start = (bf16[128,2560]{1,0:T(8,128)(2,1)}, bf16[128,2560]{1,0:T(8,128)(2,1)S(1)}, u32[]{:S(2)}, u32[]{:S(2)}) collective-permute-start(bf16[128,2560]{1,0:T(8,128)(2,1)} %get-tuple-element.34), channel_id=1, source_target_pairs={{0,1},{1,0},{2,3},{3,2},{4,5},{5,4},{6,7},{7,6},{8,9},{9,8},{10,11... | collective-permute-start | bytes 1966088 | tf_op jit(solution)/shard_map/ppermute | solution.py:247
  19.6 1.9 %collective-permute-start.1 = (bf16[128,1792]{1,0:T(8,128)(2,1)}, bf16[128,1792]{1,0:T(8,128)(2,1)}, u32[]{:S(2)}, u32[]{:S(2)}) collective-permute-start(bf16[128,1792]{1,0:T(8,128)(2,1)} %get-tuple-element.35), channel_id=1, source_target_pairs={{0,2},{1,3},{2,0},{3,1},{4,6},{5,7},{6,4},{7,5},{8,10},{9,11},{10,... | collective-permute-start | bytes 1376264 | tf_op jit(solution)/shard_map/ppermute | solution.py:247
  21.5 3.5 %collective-permute-start.2 = (bf16[128,1792]{1,0:T(8,128)(2,1)}, bf16[128,1792]{1,0:T(8,128)(2,1)}, u32[]{:S(2)}, u32[]{:S(2)}) collective-permute-start(bf16[128,1792]{1,0:T(8,128)(2,1)} %get-tuple-element.36), channel_id=1, source_target_pairs={{0,3},{1,2},{2,1},{3,0},{4,7},{5,6},{6,5},{7,4},{8,11},{9,10},{10,... | collective-permute-start | bytes 1376264 | tf_op jit(solution)/shard_map/ppermute | solution.py:247
  29.3 3.5 %all-to-all-start = ((bf16[4,256,256]{2,1,0:T(8,128)(2,1)}), bf16[4,256,256]{2,1,0:T(8,128)(2,1)S(1)}, u32[]{:S(2)}, u32[]{:S(2)}) async-start(bf16[4,256,256]{2,1,0:T(8,128)(2,1)} %copy-done.5), calls=%async_computation | async-start | bytes 1048576 | tf_op jit(solution)/shard_map/all_to_all | solution.py:263
  32.8 1.9 %collective-permute-start.3 = (bf16[128,768]{1,0:T(8,128)(2,1)}, bf16[128,768]{1,0:T(8,128)(2,1)S(1)}, u32[]{:S(2)}, u32[]{:S(2)}) collective-permute-start(bf16[128,768]{1,0:T(8,128)(2,1)} %copy-done.15), channel_id=1, source_target_pairs={{0,2},{1,3},{2,0},{3,1},{4,6},{5,7},{6,4},{7,5},{8,10},{9,11},{10,... | collective-permute-start | bytes 589832 | tf_op jit(solution)/shard_map/ppermute | solution.py:247
  34.7 3.7 %collective-permute-start.4 = (bf16[128,768]{1,0:T(8,128)(2,1)}, bf16[128,768]{1,0:T(8,128)(2,1)}, u32[]{:S(2)}, u32[]{:S(2)}) collective-permute-start(bf16[128,768]{1,0:T(8,128)(2,1)} %copy-done.14), channel_id=1, source_target_pairs={{0,3},{1,2},{2,1},{3,0},{4,7},{5,6},{6,5},{7,4},{8,11},{9,10},{10,... | collective-permute-start | bytes 589832 | tf_op jit(solution)/shard_map/ppermute | solution.py:247
  38.5 3.7 %all-to-all-done.picked = bf16[4,256,256]{2,1,0:T(8,128)(2,1)S(1)} async-done(((bf16[4,256,256]{2,1,0:T(8,128)(2,1)}), bf16[4,256,256]{2,1,0:T(8,128)(2,1)S(1)}, u32[]{:S(2)}, u32[]{:S(2)}) %all-to-all-start) | async-done | bytes 524320 | tf_op jit(solution)/shard_map/all_to_all | solution.py:263
  43.1 3.5 %all-to-all-start.1 = ((s16[4,272,256]{2,1,0:T(8,128)(2,1)}), s16[4,272,256]{2,1,0:T(8,128)(2,1)S(1)}, u32[]{:S(2)}, u32[]{:S(2)}) async-start(s16[4,272,256]{2,1,0:T(8,128)(2,1)} %shard_map.118), calls=%async_computation.1 | async-start | bytes 1114112 | tf_op jit(solution)/shard_map/all_to_all | solution.py:276
  46.6 3.0 %shard_map.112 = (s16[272,512]{1,0:T(8,128)(2,1)}, s16[544,512]{1,0:T(8,128)(2,1)}, s16[544,512]{1,0:T(8,128)(2,1)}) custom-call(bf16[128,2560]{1,0:T(8,128)(2,1)S(1)} %get-tuple-element.33.own, bf16[128,2560]{1,0:T(8,128)(2,1)S(1)} %collective-permute-done.near, bf16[128,1792]{1,0:T(8,128)(2,1)} %collective-permute-done.1.y_early, ...), custom_call_target="tpu_custom_call" | custom-call | tf_op jit(solution)/shard_map/pallas_call | solution.py:226
  50.3 8.8 %collective-permute-start.7 = (s16[272,512]{1,0:T(8,128)(2,1)}, s16[272,512]{1,0:T(8,128)(2,1)}, u32[]{:S(2)}, u32[]{:S(2)}) collective-permute-start(s16[272,512]{1,0:T(8,128)(2,1)} %get-tuple-element.46), channel_id=1, source_target_pairs={{0,8},{1,25},{2,10},{3,27},{4,12},{5,29},{6,14},{7,31},{8,16},{9,1... | collective-permute-start | bytes 835592 | tf_op jit(solution)/shard_map/ppermute | solution.py:247
  59.2 2.2 %collective-permute-start.8 = (s16[544,512]{1,0:T(8,128)(2,1)}, s16[544,512]{1,0:T(8,128)(2,1)S(1)}, u32[]{:S(2)}, u32[]{:S(2)}) collective-permute-start(s16[544,512]{1,0:T(8,128)(2,1)} %get-tuple-element.51), channel_id=1, source_target_pairs={{0,4},{1,29},{2,6},{3,31},{4,8},{5,1},{6,10},{7,3},{8,12},{9,5},{1... | collective-permute-start | bytes 1671176 | tf_op jit(solution)/shard_map/ppermute | solution.py:247
  61.4 3.1 %collective-permute-start.9 = (s16[544,512]{1,0:T(8,128)(2,1)}, s16[544,512]{1,0:T(8,128)(2,1)S(1)}, u32[]{:S(2)}, u32[]{:S(2)}) collective-permute-start(s16[544,512]{1,0:T(8,128)(2,1)} %get-tuple-element.52), channel_id=1, source_target_pairs={{0,28},{1,5},{2,30},{3,7},{4,0},{5,9},{6,2},{7,11},{8,4},{9,13},{1... | collective-permute-start | bytes 1671176 | tf_op jit(solution)/shard_map/ppermute | solution.py:247
  64.5 1.6 %copy-done.3 = bf16[1,2048,512]{2,1,0:T(8,128)(2,1)S(1)} copy-done((bf16[1,2048,512]{2,1,0:T(8,128)(2,1)S(1)}, bf16[1,2048,512]{2,1,0:T(8,128)(2,1)}, u32[]{:S(2)}) %copy-start.3) | copy-done | bytes 2097176
  68.1 2.6 %shard_map.113 = (f32[256,512]{1,0:T(8,128)S(1)}, f32[256,512]{1,0:T(8,128)S(1)}, f32[256,512]{1,0:T(8,128)S(1)}) custom-call(bf16[128,2560]{1,0:T(8,128)(2,1)S(1)} %get-tuple-element.33.own, bf16[128,2560]{1,0:T(8,128)(2,1)S(1)} %collective-permute-done.near, bf16[128,1792]{1,0:T(8,128)(2,1)} %collective-permute-done.1.y_early, ...), custom_call_target="tpu_custom_call" | custom-call | tf_op jit(solution)/shard_map/pallas_call | solution.py:226
  70.7 2.4 %collective-permute-start.5 = (f32[256,512]{1,0:T(8,128)S(1)}, f32[256,512]{1,0:T(8,128)S(1)}, u32[]{:S(2)}, u32[]{:S(2)}) collective-permute-start(f32[256,512]{1,0:T(8,128)S(1)} %get-tuple-element.42), channel_id=1, source_target_pairs={{0,1},{1,0},{2,3},{3,2},{4,5},{5,4},{6,7},{7,6},{8,9},{9,8},{10,11... | collective-permute-start | bytes 1572872 | tf_op jit(solution)/shard_map/ppermute | solution.py:247
  73.1 1.7 %shard_map.116 = (f32[256,512]{1,0:T(8,128)S(1)}, f32[256,512]{1,0:T(8,128)S(1)}) custom-call(bf16[128,2560]{1,0:T(8,128)(2,1)S(1)} %get-tuple-element.33.own, bf16[128,2560]{1,0:T(8,128)(2,1)S(1)} %collective-permute-done.near, bf16[128,1792]{1,0:T(8,128)(2,1)} %collective-permute-done.1.y_early, bf16[128,1792]{1,0:T(8,128)(2,1)} %collective-permute-done.2.x_early, ...), custom_call_target="tpu_custom_call" | custom-call | flops 14000000000 | tf_op jit(solution)/shard_map/pallas_call | solution.py:226
  74.8 3.0 %collective-permute-done.8.ahead = s16[544,512]{1,0:T(8,128)(2,1)S(1)} collective-permute-done((s16[544,512]{1,0:T(8,128)(2,1)}, s16[544,512]{1,0:T(8,128)(2,1)S(1)}, u32[]{:S(2)}, u32[]{:S(2)}) %collective-permute-start.8) | collective-permute-done | bytes 557088 | tf_op jit(solution)/shard_map/ppermute | solution.py:247
  79.4 2.1 %shard_map.117 = (s16[272,512]{1,0:T(8,128)(2,1)}, s16[272,512]{1,0:T(8,128)(2,1)}) custom-call(f32[256,512]{1,0:T(8,128)S(1)} %get-tuple-element.48.mine_ahead, f32[256,512]{1,0:T(8,128)S(1)} %get-tuple-element.49.mine_behind, s16[272,512]{1,0:T(8,128)(2,1)} %collective-permute-done.7.far, s16[544,512]{1,0:T(8,128)(2,1)S(1)} %collective-permute-done.8.ahead, ...), custom_call_target="tpu_custom_call" | custom-call | tf_op jit(solution)/shard_map/pallas_call | solution.py:226
  81.5 2.6 %collective-permute-start.10 = (s16[272,512]{1,0:T(8,128)(2,1)}, s16[272,512]{1,0:T(8,128)(2,1)S(1)}, u32[]{:S(2)}, u32[]{:S(2)}) collective-permute-start(s16[272,512]{1,0:T(8,128)(2,1)} %get-tuple-element.53), channel_id=1, source_target_pairs={{0,8},{1,25},{2,10},{3,27},{4,12},{5,29},{6,14},{7,31},{8,16},{9,1... | collective-permute-start | bytes 835592 | tf_op jit(solution)/shard_map/ppermute | solution.py:247
  84.1 3.6 %collective-permute-start.11 = (s16[272,512]{1,0:T(8,128)(2,1)}, s16[272,512]{1,0:T(8,128)(2,1)S(1)}, u32[]{:S(2)}, u32[]{:S(2)}) collective-permute-start(s16[272,512]{1,0:T(8,128)(2,1)} %get-tuple-element.54), channel_id=1, source_target_pairs={{0,24},{1,9},{2,26},{3,11},{4,28},{5,13},{6,30},{7,15},{8,0},{9,17... | collective-permute-start | bytes 835592 | tf_op jit(solution)/shard_map/ppermute | solution.py:247
  88.5 2.3 %collective-permute-start.6 = (f32[128,512]{1,0:T(8,128)}, f32[128,512]{1,0:T(8,128)S(1)}, u32[]{:S(2)}, u32[]{:S(2)}) collective-permute-start(f32[128,512]{1,0:T(8,128)} %get-tuple-element.44), channel_id=1, source_target_pairs={{0,2},{1,3},{2,0},{3,1},{4,6},{5,7},{6,4},{7,5},{8,10},{9,11},{10,... | collective-permute-start | bytes 786440 | tf_op jit(solution)/shard_map/ppermute | solution.py:247
  93.7 7.8 %collective-permute-done.11.behind2 = s16[272,512]{1,0:T(8,128)(2,1)S(1)} collective-permute-done((s16[272,512]{1,0:T(8,128)(2,1)}, s16[272,512]{1,0:T(8,128)(2,1)S(1)}, u32[]{:S(2)}, u32[]{:S(2)}) %collective-permute-start.11) | collective-permute-done | bytes 278560 | tf_op jit(solution)/shard_map/ppermute | solution.py:247
  101.5 1.8 %shard_map.120 = (f32[256,512]{1,0:T(8,128)}, bf16[256,512]{1,0:T(8,128)(2,1)}) custom-call(s32[4]{0:T(128)S(1)} %copy-done.13, f32[256,512]{1,0:T(8,128)S(1)} %copy-done.7, s16[272,512]{1,0:T(8,128)(2,1)S(1)} %collective-permute-done.10.ahead2, s16[272,512]{1,0:T(8,128)(2,1)S(1)} %collective-permute-done.11.behind2, ...), custom_call_target="tpu_custom_call" | custom-call | tf_op jit(solution)/shard_map/pallas_call | solution.py:226
  (50 shorter events, 14.5 us)
Async XLA Ops:
  7.2 17.9 %copy-start = (bf16[1,128,8192]{2,1,0:T(8,128)(2,1)S(1)}, bf16[1,128,8192]{2,1,0:T(8,128)(2,1)}, u32[]{:S(2)}) copy-start(bf16[1,128,8192]{2,1,0:T(8,128)(2,1)} %param.7) | copy-start | bytes 6291460
  7.2 17.9 %copy-start.8 = (bf16[1,128,512]{2,1,0:T(8,128)(2,1)S(1)}, bf16[1,128,512]{2,1,0:T(8,128)(2,1)}, u32[]{:S(2)}) copy-start(bf16[1,128,512]{2,1,0:T(8,128)(2,1)} %param.8) | copy-start | bytes 393220
  7.2 17.9 %copy-start.13 = (s32[4]{0:T(128)S(1)}, s32[4]{0:T(128)}, u32[]{:S(2)}) copy-start(s32[4]{0:T(128)} %frag.3) | copy-start | bytes 52
  7.2 57.3 %all-gather.3.cloned.1.call-start = ((), (), s32[]{:S(2)}) async-start(), calls=%async_computation.2 | async-start | bytes 2359296 | tf_op jit(solution)/shard_map/all_gather | solution.py:245
  10.8 35.8 %collective-permute-start = (bf16[128,2560]{1,0:T(8,128)(2,1)}, bf16[128,2560]{1,0:T(8,128)(2,1)S(1)}, u32[]{:S(2)}, u32[]{:S(2)}) collective-permute-start(bf16[128,2560]{1,0:T(8,128)(2,1)} %get-tuple-element.34), channel_id=1, source_target_pairs={{0,1},{1,0},{2,3},{3,2},{4,5},{5,4},{6,7},{7,6},{8,9},{9,8},{10,11... | collective-permute-start | bytes 1966088 | tf_op jit(solution)/shard_map/ppermute | solution.py:247
  19.6 27.0 %collective-permute-start.1 = (bf16[128,1792]{1,0:T(8,128)(2,1)}, bf16[128,1792]{1,0:T(8,128)(2,1)}, u32[]{:S(2)}, u32[]{:S(2)}) collective-permute-start(bf16[128,1792]{1,0:T(8,128)(2,1)} %get-tuple-element.35), channel_id=1, source_target_pairs={{0,2},{1,3},{2,0},{3,1},{4,6},{5,7},{6,4},{7,5},{8,10},{9,11},{10,... | collective-permute-start | bytes 1376264 | tf_op jit(solution)/shard_map/ppermute | solution.py:247
  21.5 25.1 %collective-permute-start.2 = (bf16[128,1792]{1,0:T(8,128)(2,1)}, bf16[128,1792]{1,0:T(8,128)(2,1)}, u32[]{:S(2)}, u32[]{:S(2)}) collective-permute-start(bf16[128,1792]{1,0:T(8,128)(2,1)} %get-tuple-element.36), channel_id=1, source_target_pairs={{0,3},{1,2},{2,1},{3,0},{4,7},{5,6},{6,5},{7,4},{8,11},{9,10},{10,... | collective-permute-start | bytes 1376264 | tf_op jit(solution)/shard_map/ppermute | solution.py:247
  25.1 1.0 copy-start.1
  29.3 12.8 %all-to-all-start = ((bf16[4,256,256]{2,1,0:T(8,128)(2,1)}), bf16[4,256,256]{2,1,0:T(8,128)(2,1)S(1)}, u32[]{:S(2)}, u32[]{:S(2)}) async-start(bf16[4,256,256]{2,1,0:T(8,128)(2,1)} %copy-done.5), calls=%async_computation | async-start | bytes 1048576 | tf_op jit(solution)/shard_map/all_to_all | solution.py:263
  32.8 16.9 %collective-permute-start.3 = (bf16[128,768]{1,0:T(8,128)(2,1)}, bf16[128,768]{1,0:T(8,128)(2,1)S(1)}, u32[]{:S(2)}, u32[]{:S(2)}) collective-permute-start(bf16[128,768]{1,0:T(8,128)(2,1)} %copy-done.15), channel_id=1, source_target_pairs={{0,2},{1,3},{2,0},{3,1},{4,6},{5,7},{6,4},{7,5},{8,10},{9,11},{10,... | collective-permute-start | bytes 589832 | tf_op jit(solution)/shard_map/ppermute | solution.py:247
  34.7 29.8 %collective-permute-start.4 = (bf16[128,768]{1,0:T(8,128)(2,1)}, bf16[128,768]{1,0:T(8,128)(2,1)}, u32[]{:S(2)}, u32[]{:S(2)}) collective-permute-start(bf16[128,768]{1,0:T(8,128)(2,1)} %copy-done.14), channel_id=1, source_target_pairs={{0,3},{1,2},{2,1},{3,0},{4,7},{5,6},{6,5},{7,4},{8,11},{9,10},{10,... | collective-permute-start | bytes 589832 | tf_op jit(solution)/shard_map/ppermute | solution.py:247
  43.1 47.7 %all-to-all-start.1 = ((s16[4,272,256]{2,1,0:T(8,128)(2,1)}), s16[4,272,256]{2,1,0:T(8,128)(2,1)S(1)}, u32[]{:S(2)}, u32[]{:S(2)}) async-start(s16[4,272,256]{2,1,0:T(8,128)(2,1)} %shard_map.118), calls=%async_computation.1 | async-start | bytes 1114112 | tf_op jit(solution)/shard_map/all_to_all | solution.py:276
  50.3 24.5 %collective-permute-start.7 = (s16[272,512]{1,0:T(8,128)(2,1)}, s16[272,512]{1,0:T(8,128)(2,1)}, u32[]{:S(2)}, u32[]{:S(2)}) collective-permute-start(s16[272,512]{1,0:T(8,128)(2,1)} %get-tuple-element.46), channel_id=1, source_target_pairs={{0,8},{1,25},{2,10},{3,27},{4,12},{5,29},{6,14},{7,31},{8,16},{9,1... | collective-permute-start | bytes 835592 | tf_op jit(solution)/shard_map/ppermute | solution.py:247
  59.2 18.6 %collective-permute-start.8 = (s16[544,512]{1,0:T(8,128)(2,1)}, s16[544,512]{1,0:T(8,128)(2,1)S(1)}, u32[]{:S(2)}, u32[]{:S(2)}) collective-permute-start(s16[544,512]{1,0:T(8,128)(2,1)} %get-tuple-element.51), channel_id=1, source_target_pairs={{0,4},{1,29},{2,6},{3,31},{4,8},{5,1},{6,10},{7,3},{8,12},{9,5},{1... | collective-permute-start | bytes 1671176 | tf_op jit(solution)/shard_map/ppermute | solution.py:247
  61.4 18.0 %collective-permute-start.9 = (s16[544,512]{1,0:T(8,128)(2,1)}, s16[544,512]{1,0:T(8,128)(2,1)S(1)}, u32[]{:S(2)}, u32[]{:S(2)}) collective-permute-start(s16[544,512]{1,0:T(8,128)(2,1)} %get-tuple-element.52), channel_id=1, source_target_pairs={{0,28},{1,5},{2,30},{3,7},{4,0},{5,9},{6,2},{7,11},{8,4},{9,13},{1... | collective-permute-start | bytes 1671176 | tf_op jit(solution)/shard_map/ppermute | solution.py:247
  64.5 1.6 %copy-start.3 = (bf16[1,2048,512]{2,1,0:T(8,128)(2,1)S(1)}, bf16[1,2048,512]{2,1,0:T(8,128)(2,1)}, u32[]{:S(2)}) copy-start(bf16[1,2048,512]{2,1,0:T(8,128)(2,1)} %all-gather.3.cloned.1.call-done) | copy-start | bytes 6291460
  66.1 1.0 copy-start.4
  70.7 4.1 %copy-start.6 = (f32[256,512]{1,0:T(8,128)}, f32[256,512]{1,0:T(8,128)S(1)}, u32[]{:S(2)}) copy-start(f32[256,512]{1,0:T(8,128)S(1)} %get-tuple-element.47.base) | copy-start | bytes 1572868
  70.7 17.0 %collective-permute-start.5 = (f32[256,512]{1,0:T(8,128)S(1)}, f32[256,512]{1,0:T(8,128)S(1)}, u32[]{:S(2)}, u32[]{:S(2)}) collective-permute-start(f32[256,512]{1,0:T(8,128)S(1)} %get-tuple-element.42), channel_id=1, source_target_pairs={{0,1},{1,0},{2,3},{3,2},{4,5},{5,4},{6,7},{7,6},{8,9},{9,8},{10,11... | collective-permute-start | bytes 1572872 | tf_op jit(solution)/shard_map/ppermute | solution.py:247
  79.4 22.1 %copy-start.2 = (bf16[1,256,512]{2,1,0:T(8,128)(2,1)S(1)}, bf16[1,256,512]{2,1,0:T(8,128)(2,1)}, u32[]{:S(2)}) copy-start(bf16[1,256,512]{2,1,0:T(8,128)(2,1)} %param.9) | copy-start | bytes 786436
  79.4 22.1 %copy-start.7 = (f32[256,512]{1,0:T(8,128)S(1)}, f32[256,512]{1,0:T(8,128)}, u32[]{:S(2)}) copy-start(f32[256,512]{1,0:T(8,128)} %copy-done.6) | copy-start | bytes 1572868
  81.5 12.2 %collective-permute-start.10 = (s16[272,512]{1,0:T(8,128)(2,1)}, s16[272,512]{1,0:T(8,128)(2,1)S(1)}, u32[]{:S(2)}, u32[]{:S(2)}) collective-permute-start(s16[272,512]{1,0:T(8,128)(2,1)} %get-tuple-element.53), channel_id=1, source_target_pairs={{0,8},{1,25},{2,10},{3,27},{4,12},{5,29},{6,14},{7,31},{8,16},{9,1... | collective-permute-start | bytes 835592 | tf_op jit(solution)/shard_map/ppermute | solution.py:247
  84.1 17.4 %collective-permute-start.11 = (s16[272,512]{1,0:T(8,128)(2,1)}, s16[272,512]{1,0:T(8,128)(2,1)S(1)}, u32[]{:S(2)}, u32[]{:S(2)}) collective-permute-start(s16[272,512]{1,0:T(8,128)(2,1)} %get-tuple-element.54), channel_id=1, source_target_pairs={{0,24},{1,9},{2,26},{3,11},{4,28},{5,13},{6,30},{7,15},{8,0},{9,17... | collective-permute-start | bytes 835592 | tf_op jit(solution)/shard_map/ppermute | solution.py:247
  88.5 14.8 %collective-permute-start.6 = (f32[128,512]{1,0:T(8,128)}, f32[128,512]{1,0:T(8,128)S(1)}, u32[]{:S(2)}, u32[]{:S(2)}) collective-permute-start(f32[128,512]{1,0:T(8,128)} %get-tuple-element.44), channel_id=1, source_target_pairs={{0,2},{1,3},{2,0},{3,1},{4,6},{5,7},{6,4},{7,5},{8,10},{9,11},{10,... | collective-permute-start | bytes 786440 | tf_op jit(solution)/shard_map/ppermute | solution.py:247
  (7 other events, 5.7 us)
Sparse Core Ops, SparseCore 0:
  10.1 46.0 all-gather.2

commit v3 on v2

--- a/solution.py
+++ b/solution.py
@@ -97,7 +97,7 @@
     copy_all(pairs, sems)
 
 
-def pack_late_kernel(frag, tok, cot, w, y_late, x_late, own, picked, sems):
+def pack_late_kernel(tok, cot, y_late, x_late, own, sems):
     pairs = []
     for out, k in ((y_late, 2), (x_late, 3)):
         for i in range(len(EARLY), len(DIST)):
@@ -105,6 +105,11 @@
     for i in range(len(DIST)):
         pairs.append((piece_of(tok, i, 0), own.at[:, pl.ds(column_of(i), ROWS)]))
     pairs.append((cot, own.at[:, pl.ds(SPLIT - KVH * HD, KVH * HD)]))
+    copy_all(pairs, sems)
+
+
+def pick_kernel(frag, w, picked, sems):
+    pairs = []
     for k in range(2):
         src = w.at[:, pl.ds(pl.multiple_of(frag[k] * HD, HD), HD)]
         pairs += [(src, picked.at[n, :, pl.ds(k * HD, HD)]) for n in range(NX)]
@@ -252,10 +257,10 @@
     y_early = send(y_early, swap(2))
     x_early = send(x_early, swap(3))
     near = send(near, swap(1))
-    y_late, x_late, own, picked = call(
-        pack_late_kernel,
-        [shape(TOK, WIDE - SPLIT)] * 2 + [shape(TOK, WIDE), shape(NX, ROWS, 2 * HD)],
-        fragment, tokens[0], cotangent[0], w, scalars=1, copies=2 * len(LATE) + len(DIST) + 1 + 2 * NX,
+    (picked,) = call(pick_kernel, [shape(NX, ROWS, 2 * HD)], fragment, w, scalars=1, copies=2 * NX)
+    y_late, x_late, own = call(
+        pack_late_kernel, [shape(TOK, WIDE - SPLIT)] * 2 + [shape(TOK, WIDE)],
+        tokens[0], cotangent[0], copies=2 * len(LATE) + len(DIST) + 1,
     )
     y_late = send(y_late, swap(2))
     x_late = send(x_late, swap(3))

time: 112 us -> 110 us (0.982)
  local copies, waits for them, and re-layouts: 9.23 us -> 4.55 us
  Pallas kernels: 18.5 us -> 21.2 us
    unnamed x32 -> x22, local copies, waits for them, and re-layouts: 9.23 us -> 4.55 us
    pallas_call x11 -> x12, Pallas kernels: 18.5 us -> 21.2 us  [call(): pl.pallas_call(kernel, out_shape=list(outs), in_specs=specs, out_specs=[p...]
  transfers between devices with their start and end apart: 15 -> 15, of which waited for: 4 -> 4; matrix products, arithmetic and copies ran while one was open for 0% -> 0% of each run, Pallas kernels for 16% -> 19%
where the time goes in v3:
time: 110 us; the launch traced here: 109 us
  starting transfers between devices  52 us (47%)
  Pallas kernels  21.2 us (19%)
  waiting for transfers between devices  16.7 us (15%)
  between operations  14.3 us (13%)
  local copies, waits for them, and re-layouts  4.55 us (4%)
    ppermute x12, starting transfers between devices, shards(): send = lambda x, pairs: lax.ppermute(x, 'fsdp', pairs)  44.3 us
    pallas_call x12, Pallas kernels, call(): pl.pallas_call(kernel, out_shape=list(outs), in_specs=specs, out_specs=[p...  21.2 us
    ppermute x12, waiting for transfers between devices, shards(): send = lambda x, pairs: lax.ppermute(x, 'fsdp', pairs)  13.4 us
    unnamed x22, local copies, waits for them, and re-layouts  4.55 us
    all_to_all x1, starting transfers between devices, shards(): picked = lax.all_to_all(picked, 'rep', 0, 0, axis_index_groups=x_groups())  4.15 us
    all_to_all x1, starting transfers between devices, shards(): sums = lax.all_to_all(sums, 'rep', 0, 0, axis_index_groups=y_groups())  3.47 us
    all_to_all x1, waiting for transfers between devices, shards(): picked = lax.all_to_all(picked, 'rep', 0, 0, axis_index_groups=x_groups())  2.62 us
  transfers between devices with their start and end apart: 15, of which 4 were waited for; matrix products, arithmetic and copies ran while one was open for 0% of the time, Pallas kernels for 19%

profile of v3, /device:TPU:1, one launch (start us, length us, event | category | flops | bytes accessed | tf_op | source)
XLA Modules:
  0.0 108.8 jit_solution(11608508543286944872)
XLA Ops:
  7.9 3.0 %shard_map.111 = (bf16[128,1792]{1,0:T(8,128)(2,1)}, bf16[128,1792]{1,0:T(8,128)(2,1)}, bf16[128,2560]{1,0:T(8,128)(2,1)}) custom-call(bf16[128,8192]{1,0:T(8,128)(2,1)} %bitcast.8, bf16[128,512]{1,0:T(8,128)(2,1)} %bitcast.14), custom_call_target="tpu_custom_call" | custom-call | tf_op jit(solution)/shard_map/pallas_call | solution.py:231
  10.9 8.8 %collective-permute-start = (bf16[128,2560]{1,0:T(8,128)(2,1)}, bf16[128,2560]{1,0:T(8,128)(2,1)S(1)}, u32[]{:S(2)}, u32[]{:S(2)}) collective-permute-start(bf16[128,2560]{1,0:T(8,128)(2,1)} %get-tuple-element.33), channel_id=1, source_target_pairs={{0,1},{1,0},{2,3},{3,2},{4,5},{5,4},{6,7},{7,6},{8,9},{9,8},{10,11... | collective-permute-start | bytes 1966088 | tf_op jit(solution)/shard_map/ppermute | solution.py:252
  19.7 1.9 %collective-permute-start.1 = (bf16[128,1792]{1,0:T(8,128)(2,1)}, bf16[128,1792]{1,0:T(8,128)(2,1)}, u32[]{:S(2)}, u32[]{:S(2)}) collective-permute-start(bf16[128,1792]{1,0:T(8,128)(2,1)} %get-tuple-element.34), channel_id=1, source_target_pairs={{0,2},{1,3},{2,0},{3,1},{4,6},{5,7},{6,4},{7,5},{8,10},{9,11},{10,... | collective-permute-start | bytes 1376264 | tf_op jit(solution)/shard_map/ppermute | solution.py:252
  21.6 3.5 %collective-permute-start.2 = (bf16[128,1792]{1,0:T(8,128)(2,1)}, bf16[128,1792]{1,0:T(8,128)(2,1)}, u32[]{:S(2)}, u32[]{:S(2)}) collective-permute-start(bf16[128,1792]{1,0:T(8,128)(2,1)} %get-tuple-element.35), channel_id=1, source_target_pairs={{0,3},{1,2},{2,1},{3,0},{4,7},{5,6},{6,5},{7,4},{8,11},{9,10},{10,... | collective-permute-start | bytes 1376264 | tf_op jit(solution)/shard_map/ppermute | solution.py:252
  26.7 4.2 %all-to-all-start = ((bf16[4,256,256]{2,1,0:T(8,128)(2,1)}), bf16[4,256,256]{2,1,0:T(8,128)(2,1)}, u32[]{:S(2)}, u32[]{:S(2)}) async-start(bf16[4,256,256]{2,1,0:T(8,128)(2,1)} %shard_map.118), calls=%async_computation | async-start | bytes 1048576 | tf_op jit(solution)/shard_map/all_to_all | solution.py:268
  32.0 1.9 %collective-permute-start.3 = (bf16[128,768]{1,0:T(8,128)(2,1)}, bf16[128,768]{1,0:T(8,128)(2,1)S(1)}, u32[]{:S(2)}, u32[]{:S(2)}) collective-permute-start(bf16[128,768]{1,0:T(8,128)(2,1)} %get-tuple-element.37), channel_id=1, source_target_pairs={{0,2},{1,3},{2,0},{3,1},{4,6},{5,7},{6,4},{7,5},{8,10},{9,11},{10,... | collective-permute-start | bytes 589832 | tf_op jit(solution)/shard_map/ppermute | solution.py:252
  34.0 3.7 %collective-permute-start.4 = (bf16[128,768]{1,0:T(8,128)(2,1)}, bf16[128,768]{1,0:T(8,128)(2,1)}, u32[]{:S(2)}, u32[]{:S(2)}) collective-permute-start(bf16[128,768]{1,0:T(8,128)(2,1)} %get-tuple-element.39), channel_id=1, source_target_pairs={{0,3},{1,2},{2,1},{3,0},{4,7},{5,6},{6,5},{7,4},{8,11},{9,10},{10,... | collective-permute-start | bytes 589832 | tf_op jit(solution)/shard_map/ppermute | solution.py:252
  37.7 2.6 %all-to-all-done.picked = bf16[4,256,256]{2,1,0:T(8,128)(2,1)} async-done(((bf16[4,256,256]{2,1,0:T(8,128)(2,1)}), bf16[4,256,256]{2,1,0:T(8,128)(2,1)}, u32[]{:S(2)}, u32[]{:S(2)}) %all-to-all-start) | async-done | bytes 524320 | tf_op jit(solution)/shard_map/all_to_all | solution.py:268
  40.3 2.0 %shard_map.119 = s16[4,272,256]{2,1,0:T(8,128)(2,1)} custom-call(bf16[4,256,256]{2,1,0:T(8,128)(2,1)} %all-to-all-done.picked), custom_call_target="tpu_custom_call" | custom-call | tf_op jit(solution)/shard_map/pallas_call | solution.py:231
  42.3 3.5 %all-to-all-start.1 = ((s16[4,272,256]{2,1,0:T(8,128)(2,1)}), s16[4,272,256]{2,1,0:T(8,128)(2,1)S(1)}, u32[]{:S(2)}, u32[]{:S(2)}) async-start(s16[4,272,256]{2,1,0:T(8,128)(2,1)} %shard_map.119), calls=%async_computation.1 | async-start | bytes 1114112 | tf_op jit(solution)/shard_map/all_to_all | solution.py:281
  45.8 3.0 %shard_map.112 = (s16[272,512]{1,0:T(8,128)(2,1)}, s16[544,512]{1,0:T(8,128)(2,1)}, s16[544,512]{1,0:T(8,128)(2,1)}) custom-call(bf16[128,2560]{1,0:T(8,128)(2,1)S(1)} %get-tuple-element.32.own, bf16[128,2560]{1,0:T(8,128)(2,1)S(1)} %collective-permute-done.near, bf16[128,1792]{1,0:T(8,128)(2,1)} %collective-permute-done.1.y_early, ...), custom_call_target="tpu_custom_call" | custom-call | tf_op jit(solution)/shard_map/pallas_call | solution.py:231
  48.9 8.4 %collective-permute-start.7 = (s16[272,512]{1,0:T(8,128)(2,1)}, s16[272,512]{1,0:T(8,128)(2,1)}, u32[]{:S(2)}, u32[]{:S(2)}) collective-permute-start(s16[272,512]{1,0:T(8,128)(2,1)} %get-tuple-element.45), channel_id=1, source_target_pairs={{0,8},{1,25},{2,10},{3,27},{4,12},{5,29},{6,14},{7,31},{8,16},{9,1... | collective-permute-start | bytes 835592 | tf_op jit(solution)/shard_map/ppermute | solution.py:252
  57.3 2.2 %collective-permute-start.8 = (s16[544,512]{1,0:T(8,128)(2,1)}, s16[544,512]{1,0:T(8,128)(2,1)S(1)}, u32[]{:S(2)}, u32[]{:S(2)}) collective-permute-start(s16[544,512]{1,0:T(8,128)(2,1)} %get-tuple-element.50), channel_id=1, source_target_pairs={{0,4},{1,29},{2,6},{3,31},{4,8},{5,1},{6,10},{7,3},{8,12},{9,5},{1... | collective-permute-start | bytes 1671176 | tf_op jit(solution)/shard_map/ppermute | solution.py:252
  59.5 3.1 %collective-permute-start.9 = (s16[544,512]{1,0:T(8,128)(2,1)}, s16[544,512]{1,0:T(8,128)(2,1)S(1)}, u32[]{:S(2)}, u32[]{:S(2)}) collective-permute-start(s16[544,512]{1,0:T(8,128)(2,1)} %get-tuple-element.51), channel_id=1, source_target_pairs={{0,28},{1,5},{2,30},{3,7},{4,0},{5,9},{6,2},{7,11},{8,4},{9,13},{1... | collective-permute-start | bytes 1671176 | tf_op jit(solution)/shard_map/ppermute | solution.py:252
  65.2 2.6 %shard_map.113 = (f32[256,512]{1,0:T(8,128)S(1)}, f32[256,512]{1,0:T(8,128)S(1)}, f32[256,512]{1,0:T(8,128)S(1)}) custom-call(bf16[128,2560]{1,0:T(8,128)(2,1)S(1)} %get-tuple-element.32.own, bf16[128,2560]{1,0:T(8,128)(2,1)S(1)} %collective-permute-done.near, bf16[128,1792]{1,0:T(8,128)(2,1)} %collective-permute-done.1.y_early, ...), custom_call_target="tpu_custom_call" | custom-call | tf_op jit(solution)/shard_map/pallas_call | solution.py:231
  67.9 2.3 %collective-permute-start.5 = (f32[256,512]{1,0:T(8,128)S(1)}, f32[256,512]{1,0:T(8,128)S(1)}, u32[]{:S(2)}, u32[]{:S(2)}) collective-permute-start(f32[256,512]{1,0:T(8,128)S(1)} %get-tuple-element.41), channel_id=1, source_target_pairs={{0,1},{1,0},{2,3},{3,2},{4,5},{5,4},{6,7},{7,6},{8,9},{9,8},{10,11... | collective-permute-start | bytes 1572872 | tf_op jit(solution)/shard_map/ppermute | solution.py:252
  70.2 1.7 %shard_map.116 = (f32[256,512]{1,0:T(8,128)S(1)}, f32[256,512]{1,0:T(8,128)S(1)}) custom-call(bf16[128,2560]{1,0:T(8,128)(2,1)S(1)} %get-tuple-element.32.own, bf16[128,2560]{1,0:T(8,128)(2,1)S(1)} %collective-permute-done.near, bf16[128,1792]{1,0:T(8,128)(2,1)} %collective-permute-done.1.y_early, bf16[128,1792]{1,0:T(8,128)(2,1)} %collective-permute-done.2.x_early, ...), custom_call_target="tpu_custom_call" | custom-call | flops 14000000000 | tf_op jit(solution)/shard_map/pallas_call | solution.py:231
  71.9 4.5 %collective-permute-done.8.ahead = s16[544,512]{1,0:T(8,128)(2,1)S(1)} collective-permute-done((s16[544,512]{1,0:T(8,128)(2,1)}, s16[544,512]{1,0:T(8,128)(2,1)S(1)}, u32[]{:S(2)}, u32[]{:S(2)}) %collective-permute-start.8) | collective-permute-done | bytes 557088 | tf_op jit(solution)/shard_map/ppermute | solution.py:252
  77.5 2.1 %shard_map.117 = (s16[272,512]{1,0:T(8,128)(2,1)}, s16[272,512]{1,0:T(8,128)(2,1)}) custom-call(f32[256,512]{1,0:T(8,128)S(1)} %get-tuple-element.47.mine_ahead, f32[256,512]{1,0:T(8,128)S(1)} %get-tuple-element.48.mine_behind, s16[272,512]{1,0:T(8,128)(2,1)} %collective-permute-done.7.far, s16[544,512]{1,0:T(8,128)(2,1)S(1)} %collective-permute-done.8.ahead, ...), custom_call_target="tpu_custom_call" | custom-call | tf_op jit(solution)/shard_map/pallas_call | solution.py:231
  79.6 2.5 %collective-permute-start.10 = (s16[272,512]{1,0:T(8,128)(2,1)}, s16[272,512]{1,0:T(8,128)(2,1)S(1)}, u32[]{:S(2)}, u32[]{:S(2)}) collective-permute-start(s16[272,512]{1,0:T(8,128)(2,1)} %get-tuple-element.52), channel_id=1, source_target_pairs={{0,8},{1,25},{2,10},{3,27},{4,12},{5,29},{6,14},{7,31},{8,16},{9,1... | collective-permute-start | bytes 835592 | tf_op jit(solution)/shard_map/ppermute | solution.py:252
  82.1 3.7 %collective-permute-start.11 = (s16[272,512]{1,0:T(8,128)(2,1)}, s16[272,512]{1,0:T(8,128)(2,1)S(1)}, u32[]{:S(2)}, u32[]{:S(2)}) collective-permute-start(s16[272,512]{1,0:T(8,128)(2,1)} %get-tuple-element.53), channel_id=1, source_target_pairs={{0,24},{1,9},{2,26},{3,11},{4,28},{5,13},{6,30},{7,15},{8,0},{9,17... | collective-permute-start | bytes 835592 | tf_op jit(solution)/shard_map/ppermute | solution.py:252
  86.5 2.3 %collective-permute-start.6 = (f32[128,512]{1,0:T(8,128)}, f32[128,512]{1,0:T(8,128)S(1)}, u32[]{:S(2)}, u32[]{:S(2)}) collective-permute-start(f32[128,512]{1,0:T(8,128)} %get-tuple-element.43), channel_id=1, source_target_pairs={{0,2},{1,3},{2,0},{3,1},{4,6},{5,7},{6,4},{7,5},{8,10},{9,11},{10,... | collective-permute-start | bytes 786440 | tf_op jit(solution)/shard_map/ppermute | solution.py:252
  91.8 7.8 %collective-permute-done.11.behind2 = s16[272,512]{1,0:T(8,128)(2,1)S(1)} collective-permute-done((s16[272,512]{1,0:T(8,128)(2,1)}, s16[272,512]{1,0:T(8,128)(2,1)S(1)}, u32[]{:S(2)}, u32[]{:S(2)}) %collective-permute-start.11) | collective-permute-done | bytes 278560 | tf_op jit(solution)/shard_map/ppermute | solution.py:252
  99.5 1.8 %shard_map.121 = (f32[256,512]{1,0:T(8,128)}, bf16[256,512]{1,0:T(8,128)(2,1)}) custom-call(s32[4]{0:T(128)S(1)} %copy-done.10, f32[256,512]{1,0:T(8,128)S(1)} %copy-done.7, s16[272,512]{1,0:T(8,128)(2,1)S(1)} %collective-permute-done.10.ahead2, s16[272,512]{1,0:T(8,128)(2,1)S(1)} %collective-permute-done.11.behind2, ...), custom_call_target="tpu_custom_call" | custom-call | tf_op jit(solution)/shard_map/pallas_call | solution.py:231
  (41 shorter events, 11.6 us)
Async XLA Ops:
  7.2 18.0 %copy-start.1 = (bf16[1,256,512]{2,1,0:T(8,128)(2,1)S(1)}, bf16[1,256,512]{2,1,0:T(8,128)(2,1)}, u32[]{:S(2)}) copy-start(bf16[1,256,512]{2,1,0:T(8,128)(2,1)} %param.9) | copy-start | bytes 786436
  7.2 18.0 %copy-start.10 = (s32[4]{0:T(128)S(1)}, s32[4]{0:T(128)}, u32[]{:S(2)}) copy-start(s32[4]{0:T(128)} %frag.3) | copy-start | bytes 52
  7.2 55.4 %all-gather.3.cloned.1.call-start = ((), (), s32[]{:S(2)}) async-start(), calls=%async_computation.2 | async-start | bytes 2359296 | tf_op jit(solution)/shard_map/all_gather | solution.py:250
  7.9 23.0 %copy-start = (bf16[1,128,8192]{2,1,0:T(8,128)(2,1)S(1)}, bf16[1,128,8192]{2,1,0:T(8,128)(2,1)}, u32[]{:S(2)}) copy-start(bf16[1,128,8192]{2,1,0:T(8,128)(2,1)} %param.7) | copy-start | bytes 6291460
  7.9 23.0 %copy-start.5 = (bf16[1,128,512]{2,1,0:T(8,128)(2,1)S(1)}, bf16[1,128,512]{2,1,0:T(8,128)(2,1)}, u32[]{:S(2)}) copy-start(bf16[1,128,512]{2,1,0:T(8,128)(2,1)} %param.8) | copy-start | bytes 393220
  10.9 34.9 %collective-permute-start = (bf16[128,2560]{1,0:T(8,128)(2,1)}, bf16[128,2560]{1,0:T(8,128)(2,1)S(1)}, u32[]{:S(2)}, u32[]{:S(2)}) collective-permute-start(bf16[128,2560]{1,0:T(8,128)(2,1)} %get-tuple-element.33), channel_id=1, source_target_pairs={{0,1},{1,0},{2,3},{3,2},{4,5},{5,4},{6,7},{7,6},{8,9},{9,8},{10,11... | collective-permute-start | bytes 1966088 | tf_op jit(solution)/shard_map/ppermute | solution.py:252
  19.7 26.1 %collective-permute-start.1 = (bf16[128,1792]{1,0:T(8,128)(2,1)}, bf16[128,1792]{1,0:T(8,128)(2,1)}, u32[]{:S(2)}, u32[]{:S(2)}) collective-permute-start(bf16[128,1792]{1,0:T(8,128)(2,1)} %get-tuple-element.34), channel_id=1, source_target_pairs={{0,2},{1,3},{2,0},{3,1},{4,6},{5,7},{6,4},{7,5},{8,10},{9,11},{10,... | collective-permute-start | bytes 1376264 | tf_op jit(solution)/shard_map/ppermute | solution.py:252
  21.6 24.2 %collective-permute-start.2 = (bf16[128,1792]{1,0:T(8,128)(2,1)}, bf16[128,1792]{1,0:T(8,128)(2,1)}, u32[]{:S(2)}, u32[]{:S(2)}) collective-permute-start(bf16[128,1792]{1,0:T(8,128)(2,1)} %get-tuple-element.35), channel_id=1, source_target_pairs={{0,3},{1,2},{2,1},{3,0},{4,7},{5,6},{6,5},{7,4},{8,11},{9,10},{10,... | collective-permute-start | bytes 1376264 | tf_op jit(solution)/shard_map/ppermute | solution.py:252
  26.7 13.6 %all-to-all-start = ((bf16[4,256,256]{2,1,0:T(8,128)(2,1)}), bf16[4,256,256]{2,1,0:T(8,128)(2,1)}, u32[]{:S(2)}, u32[]{:S(2)}) async-start(bf16[4,256,256]{2,1,0:T(8,128)(2,1)} %shard_map.118), calls=%async_computation | async-start | bytes 1048576 | tf_op jit(solution)/shard_map/all_to_all | solution.py:268
  32.0 16.9 %collective-permute-start.3 = (bf16[128,768]{1,0:T(8,128)(2,1)}, bf16[128,768]{1,0:T(8,128)(2,1)S(1)}, u32[]{:S(2)}, u32[]{:S(2)}) collective-permute-start(bf16[128,768]{1,0:T(8,128)(2,1)} %get-tuple-element.37), channel_id=1, source_target_pairs={{0,2},{1,3},{2,0},{3,1},{4,6},{5,7},{6,4},{7,5},{8,10},{9,11},{10,... | collective-permute-start | bytes 589832 | tf_op jit(solution)/shard_map/ppermute | solution.py:252
  34.0 28.6 %collective-permute-start.4 = (bf16[128,768]{1,0:T(8,128)(2,1)}, bf16[128,768]{1,0:T(8,128)(2,1)}, u32[]{:S(2)}, u32[]{:S(2)}) collective-permute-start(bf16[128,768]{1,0:T(8,128)(2,1)} %get-tuple-element.39), channel_id=1, source_target_pairs={{0,3},{1,2},{2,1},{3,0},{4,7},{5,6},{6,5},{7,4},{8,11},{9,10},{10,... | collective-permute-start | bytes 589832 | tf_op jit(solution)/shard_map/ppermute | solution.py:252
  42.3 46.5 %all-to-all-start.1 = ((s16[4,272,256]{2,1,0:T(8,128)(2,1)}), s16[4,272,256]{2,1,0:T(8,128)(2,1)S(1)}, u32[]{:S(2)}, u32[]{:S(2)}) async-start(s16[4,272,256]{2,1,0:T(8,128)(2,1)} %shard_map.119), calls=%async_computation.1 | async-start | bytes 1114112 | tf_op jit(solution)/shard_map/all_to_all | solution.py:281
  48.9 22.9 %collective-permute-start.7 = (s16[272,512]{1,0:T(8,128)(2,1)}, s16[272,512]{1,0:T(8,128)(2,1)}, u32[]{:S(2)}, u32[]{:S(2)}) collective-permute-start(s16[272,512]{1,0:T(8,128)(2,1)} %get-tuple-element.45), channel_id=1, source_target_pairs={{0,8},{1,25},{2,10},{3,27},{4,12},{5,29},{6,14},{7,31},{8,16},{9,1... | collective-permute-start | bytes 835592 | tf_op jit(solution)/shard_map/ppermute | solution.py:252
  57.3 19.0 %collective-permute-start.8 = (s16[544,512]{1,0:T(8,128)(2,1)}, s16[544,512]{1,0:T(8,128)(2,1)S(1)}, u32[]{:S(2)}, u32[]{:S(2)}) collective-permute-start(s16[544,512]{1,0:T(8,128)(2,1)} %get-tuple-element.50), channel_id=1, source_target_pairs={{0,4},{1,29},{2,6},{3,31},{4,8},{5,1},{6,10},{7,3},{8,12},{9,5},{1... | collective-permute-start | bytes 1671176 | tf_op jit(solution)/shard_map/ppermute | solution.py:252
  59.5 18.0 %collective-permute-start.9 = (s16[544,512]{1,0:T(8,128)(2,1)}, s16[544,512]{1,0:T(8,128)(2,1)S(1)}, u32[]{:S(2)}, u32[]{:S(2)}) collective-permute-start(s16[544,512]{1,0:T(8,128)(2,1)} %get-tuple-element.51), channel_id=1, source_target_pairs={{0,28},{1,5},{2,30},{3,7},{4,0},{5,9},{6,2},{7,11},{8,4},{9,13},{1... | collective-permute-start | bytes 1671176 | tf_op jit(solution)/shard_map/ppermute | solution.py:252
  62.6 1.6 %copy-start.3 = (bf16[1,2048,512]{2,1,0:T(8,128)(2,1)S(1)}, bf16[1,2048,512]{2,1,0:T(8,128)(2,1)}, u32[]{:S(2)}) copy-start(bf16[1,2048,512]{2,1,0:T(8,128)(2,1)} %all-gather.3.cloned.1.call-done) | copy-start | bytes 6291460
  64.2 1.0 copy-start.4
  67.8 4.0 %copy-start.6 = (f32[256,512]{1,0:T(8,128)}, f32[256,512]{1,0:T(8,128)S(1)}, u32[]{:S(2)}) copy-start(f32[256,512]{1,0:T(8,128)S(1)} %get-tuple-element.46.base) | copy-start | bytes 1572868
  67.9 17.9 %collective-permute-start.5 = (f32[256,512]{1,0:T(8,128)S(1)}, f32[256,512]{1,0:T(8,128)S(1)}, u32[]{:S(2)}, u32[]{:S(2)}) collective-permute-start(f32[256,512]{1,0:T(8,128)S(1)} %get-tuple-element.41), channel_id=1, source_target_pairs={{0,1},{1,0},{2,3},{3,2},{4,5},{5,4},{6,7},{7,6},{8,9},{9,8},{10,11... | collective-permute-start | bytes 1572872 | tf_op jit(solution)/shard_map/ppermute | solution.py:252
  77.5 22.1 %copy-start.2 = (bf16[1,256,512]{2,1,0:T(8,128)(2,1)S(1)}, bf16[1,256,512]{2,1,0:T(8,128)(2,1)}, u32[]{:S(2)}) copy-start(bf16[1,256,512]{2,1,0:T(8,128)(2,1)} %param.9) | copy-start | bytes 786436
  77.5 22.1 %copy-start.7 = (f32[256,512]{1,0:T(8,128)S(1)}, f32[256,512]{1,0:T(8,128)}, u32[]{:S(2)}) copy-start(f32[256,512]{1,0:T(8,128)} %copy-done.6) | copy-start | bytes 1572868
  79.6 12.2 %collective-permute-start.10 = (s16[272,512]{1,0:T(8,128)(2,1)}, s16[272,512]{1,0:T(8,128)(2,1)S(1)}, u32[]{:S(2)}, u32[]{:S(2)}) collective-permute-start(s16[272,512]{1,0:T(8,128)(2,1)} %get-tuple-element.52), channel_id=1, source_target_pairs={{0,8},{1,25},{2,10},{3,27},{4,12},{5,29},{6,14},{7,31},{8,16},{9,1... | collective-permute-start | bytes 835592 | tf_op jit(solution)/shard_map/ppermute | solution.py:252
  82.1 17.4 %collective-permute-start.11 = (s16[272,512]{1,0:T(8,128)(2,1)}, s16[272,512]{1,0:T(8,128)(2,1)S(1)}, u32[]{:S(2)}, u32[]{:S(2)}) collective-permute-start(s16[272,512]{1,0:T(8,128)(2,1)} %get-tuple-element.53), channel_id=1, source_target_pairs={{0,24},{1,9},{2,26},{3,11},{4,28},{5,13},{6,30},{7,15},{8,0},{9,17... | collective-permute-start | bytes 835592 | tf_op jit(solution)/shard_map/ppermute | solution.py:252
  86.5 14.8 %collective-permute-start.6 = (f32[128,512]{1,0:T(8,128)}, f32[128,512]{1,0:T(8,128)S(1)}, u32[]{:S(2)}, u32[]{:S(2)}) collective-permute-start(f32[128,512]{1,0:T(8,128)} %get-tuple-element.43), channel_id=1, source_target_pairs={{0,2},{1,3},{2,0},{3,1},{4,6},{5,7},{6,4},{7,5},{8,10},{9,11},{10,... | collective-permute-start | bytes 786440 | tf_op jit(solution)/shard_map/ppermute | solution.py:252
  (2 other events, 1.9 us)
Sparse Core Ops, SparseCore 0:
  10.1 46.4 all-gather.2

commit v4 on v3

--- a/solution.py
+++ b/solution.py
@@ -32,7 +32,8 @@
 SPLIT = len(EARLY) * ROWS + KVH * HD
 WIDE = SPLIT + len(LATE) * ROWS
 LEVELS = 32000.0
-CODED = ROWS + 16
+GROUP = 16
+CODED = ROWS + GROUP
 
 
 def place(z, y, c):
@@ -116,18 +117,33 @@
     copy_all(pairs, sems)
 
 
-def encode(x, out, at=0):
+def levels_of(x):
     top = jnp.max(jnp.abs(x), axis=0, keepdims=True)
     power = jnp.ceil(jnp.log2(jnp.maximum(top, 1e-30)))
-    out[at : at + ROWS, :] = jnp.round(x * (LEVELS * jnp.exp2(-power))).astype(jnp.int32).astype(jnp.int16)
-    out[at + ROWS : at + CODED, :] = (
-        jnp.broadcast_to(power, (CODED - ROWS, x.shape[1])).astype(jnp.int32).astype(jnp.int16)
-    )
-
-
-def decode(ref, at=0):
-    power = ref[at + ROWS : at + CODED, :].astype(jnp.int32).astype(F32)[0:1]
-    return ref[at : at + ROWS, :].astype(jnp.int32).astype(F32) * (jnp.exp2(power) * (1.0 / LEVELS))
+    return jnp.round(x * (LEVELS * jnp.exp2(-power))).astype(jnp.int32).astype(jnp.int16), power
+
+
+def encode(x, out):
+    coded, power = levels_of(x)
+    out[:ROWS, :] = coded
+    out[ROWS:, :] = jnp.broadcast_to(power, (GROUP, x.shape[1])).astype(jnp.int32).astype(jnp.int16)
+
+
+def encode_pair(x, y, out):
+    coded_x, power_x = levels_of(x)
+    coded_y, power_y = levels_of(y)
+    out[:ROWS, :] = coded_x
+    out[ROWS : 2 * ROWS, :] = coded_y
+    half = (GROUP // 2, x.shape[1])
+    powers = jnp.concatenate([jnp.broadcast_to(power_x, half), jnp.broadcast_to(power_y, half)], axis=0)
+    out[2 * ROWS :, :] = powers.astype(jnp.int32).astype(jnp.int16)
+
+
+def decode(ref, at=0, blocks=1):
+    powers = ref[blocks * ROWS :, :].astype(jnp.int32).astype(F32)
+    row = at * (GROUP // blocks)
+    scale = jnp.exp2(powers[row : row + 1]) * (1.0 / LEVELS)
+    return ref[at * ROWS : (at + 1) * ROWS, :].astype(jnp.int32).astype(F32) * scale
 
 
 def partial_grad(refs, cot, dist):
@@ -151,10 +167,8 @@
     refs = [(r, None) for r in (own, near, y_early, x_early)]
     cot = cotangents(refs)
     encode(partial_grad(refs, cot, 4), far)
-    encode(partial_grad(refs, cot, 3), ahead)
-    encode(partial_grad(refs, cot, 1), ahead, CODED)
-    encode(partial_grad(refs, cot, -3), behind)
-    encode(partial_grad(refs, cot, -1), behind, CODED)
+    encode_pair(partial_grad(refs, cot, 3), partial_grad(refs, cot, 1), ahead)
+    encode_pair(partial_grad(refs, cot, -3), partial_grad(refs, cot, -1), behind)
 
 
 def late_kernel(own, near, y_early, x_early, y_late, x_late, ahead2, behind2):
@@ -165,8 +179,8 @@
 
 
 def relay_kernel(mine_ahead, mine_behind, far, ahead, behind, ahead2, behind2):
-    encode(mine_ahead[...] + decode(far) + decode(ahead), ahead2)
-    encode(mine_behind[...] + decode(behind), behind2)
+    encode(mine_ahead[...] + decode(far) + decode(ahead, 0, 2), ahead2)
+    encode(mine_behind[...] + decode(behind, 0, 2), behind2)
 
 
 def key_kernel(own, near, y_early, x_early, y_late, x_late, w, moment, base, kept, sent):
@@ -203,7 +217,7 @@
 
 
 def update_kernel(frag, base, ahead2, behind2, ahead, behind, w, blend, moment_new, weight_new):
-    others = decode(ahead2) + decode(behind2) + decode(ahead, CODED) + decode(behind, CODED)
+    others = decode(ahead2) + decode(behind2) + decode(ahead, 1, 2) + decode(behind, 1, 2)
     new = base[...] + others * (D ** -0.5)
     moment_new[...] = new
     inner = w[...].astype(F32) - LR_INNER * new
@@ -268,7 +282,7 @@
     picked = lax.all_to_all(picked, "rep", 0, 0, axis_index_groups=x_groups())
 
     one = shape(CODED, width, kind=jnp.int16)
-    two = shape(2 * CODED, width, kind=jnp.int16)
+    two = shape(2 * ROWS + GROUP, width, kind=jnp.int16)
     wide = shape(ROWS, width, kind=F32)
     far, ahead, behind = call(early_kernel, [one, two, two], own, near, y_early, x_early)
     far, y_late = lax.optimization_barrier((far, y_late))
@@ -288,7 +302,7 @@
     half = shape(TOK, width, kind=F32)
     mine_key, theirs_key = call(key_half_kernel, [half] * 2, kept, send(sent, swap(1)))
     base, far = lax.optimization_barrier((base, far))
-    ahead2, behind2 = call(relay_kernel, [one] * 2, *mine, far, ahead, behind)
+    ahead2, behind2 = call(relay_kernel, [one] * 2, *mine, far, ahead, behind, hint=12)
     ahead2 = send(ahead2, ring(2))
     behind2 = send(behind2, ring(-2))
     (key_out,) = call(key_sum_kernel, [shape(TOK, width)], mine_key, send(theirs_key, swap(2)))

time: 110 us -> 109 us (level)
  waiting for transfers between devices: 16.7 us -> 14.8 us
  local copies, waits for them, and re-layouts: 4.55 us -> 6.15 us
    ppermute x12, waiting for transfers between devices: 13.4 us -> 11.5 us  [shards(): send = lambda x, pairs: lax.ppermute(x, 'fsdp', pairs)]
    unnamed x22 -> x30, local copies, waits for them, and re-layouts: 4.55 us -> 6.15 us
where the time goes in v4:
time: 109 us
  starting transfers between devices  52.2 us (48%)
  Pallas kernels  21.1 us (19%)
  waiting for transfers between devices  14.8 us (14%)
  between operations  14.3 us (13%)
  local copies, waits for them, and re-layouts  6.15 us (6%)
    ppermute x12, starting transfers between devices, shards(): send = lambda x, pairs: lax.ppermute(x, 'fsdp', pairs)  44.5 us
    pallas_call x12, Pallas kernels, call(): pl.pallas_call(kernel, out_shape=list(outs), in_specs=specs, out_specs=[p...  21.1 us
    ppermute x12, waiting for transfers between devices, shards(): send = lambda x, pairs: lax.ppermute(x, 'fsdp', pairs)  11.5 us
    unnamed x30, local copies, waits for them, and re-layouts  6.15 us
    all_to_all x1, starting transfers between devices, shards(): picked = lax.all_to_all(picked, 'rep', 0, 0, axis_index_groups=x_groups())  4.17 us
    all_to_all x1, starting transfers between devices, shards(): sums = lax.all_to_all(sums, 'rep', 0, 0, axis_index_groups=y_groups())  3.47 us
    all_to_all x1, waiting for transfers between devices, shards(): picked = lax.all_to_all(picked, 'rep', 0, 0, axis_index_groups=x_groups())  2.63 us
  transfers between devices with their start and end apart: 15, of which 4 were waited for; matrix products, arithmetic and copies ran while one was open for 0% of the time, Pallas kernels for 19%

profile of v4, /device:TPU:1, one launch (start us, length us, event | category | flops | bytes accessed | tf_op | source)
XLA Modules:
  0.0 108.6 jit_solution(982041909309233563)
XLA Ops:
  7.9 3.0 %shard_map.111 = (bf16[128,1792]{1,0:T(8,128)(2,1)}, bf16[128,1792]{1,0:T(8,128)(2,1)}, bf16[128,2560]{1,0:T(8,128)(2,1)}) custom-call(bf16[128,8192]{1,0:T(8,128)(2,1)} %bitcast.8, bf16[128,512]{1,0:T(8,128)(2,1)} %bitcast.14), custom_call_target="tpu_custom_call" | custom-call | tf_op jit(solution)/shard_map/pallas_call | solution.py:245
  10.9 8.8 %collective-permute-start = (bf16[128,2560]{1,0:T(8,128)(2,1)}, bf16[128,2560]{1,0:T(8,128)(2,1)S(1)}, u32[]{:S(2)}, u32[]{:S(2)}) collective-permute-start(bf16[128,2560]{1,0:T(8,128)(2,1)} %get-tuple-element.33), channel_id=1, source_target_pairs={{0,1},{1,0},{2,3},{3,2},{4,5},{5,4},{6,7},{7,6},{8,9},{9,8},{10,11... | collective-permute-start | bytes 1966088 | tf_op jit(solution)/shard_map/ppermute | solution.py:266
  19.7 1.9 %collective-permute-start.1 = (bf16[128,1792]{1,0:T(8,128)(2,1)}, bf16[128,1792]{1,0:T(8,128)(2,1)}, u32[]{:S(2)}, u32[]{:S(2)}) collective-permute-start(bf16[128,1792]{1,0:T(8,128)(2,1)} %get-tuple-element.34), channel_id=1, source_target_pairs={{0,2},{1,3},{2,0},{3,1},{4,6},{5,7},{6,4},{7,5},{8,10},{9,11},{10,... | collective-permute-start | bytes 1376264 | tf_op jit(solution)/shard_map/ppermute | solution.py:266
  21.6 3.5 %collective-permute-start.2 = (bf16[128,1792]{1,0:T(8,128)(2,1)}, bf16[128,1792]{1,0:T(8,128)(2,1)}, u32[]{:S(2)}, u32[]{:S(2)}) collective-permute-start(bf16[128,1792]{1,0:T(8,128)(2,1)} %get-tuple-element.35), channel_id=1, source_target_pairs={{0,3},{1,2},{2,1},{3,0},{4,7},{5,6},{6,5},{7,4},{8,11},{9,10},{10,... | collective-permute-start | bytes 1376264 | tf_op jit(solution)/shard_map/ppermute | solution.py:266
  26.7 4.2 %all-to-all-start = ((bf16[4,256,256]{2,1,0:T(8,128)(2,1)}), bf16[4,256,256]{2,1,0:T(8,128)(2,1)}, u32[]{:S(2)}, u32[]{:S(2)}) async-start(bf16[4,256,256]{2,1,0:T(8,128)(2,1)} %shard_map.118), calls=%async_computation | async-start | bytes 1048576 | tf_op jit(solution)/shard_map/all_to_all | solution.py:282
  32.1 1.9 %collective-permute-start.3 = (bf16[128,768]{1,0:T(8,128)(2,1)}, bf16[128,768]{1,0:T(8,128)(2,1)S(1)}, u32[]{:S(2)}, u32[]{:S(2)}) collective-permute-start(bf16[128,768]{1,0:T(8,128)(2,1)} %get-tuple-element.37), channel_id=1, source_target_pairs={{0,2},{1,3},{2,0},{3,1},{4,6},{5,7},{6,4},{7,5},{8,10},{9,11},{10,... | collective-permute-start | bytes 589832 | tf_op jit(solution)/shard_map/ppermute | solution.py:266
  34.0 3.7 %collective-permute-start.4 = (bf16[128,768]{1,0:T(8,128)(2,1)}, bf16[128,768]{1,0:T(8,128)(2,1)S(1)}, u32[]{:S(2)}, u32[]{:S(2)}) collective-permute-start(bf16[128,768]{1,0:T(8,128)(2,1)} %get-tuple-element.39), channel_id=1, source_target_pairs={{0,3},{1,2},{2,1},{3,0},{4,7},{5,6},{6,5},{7,4},{8,11},{9,10},{10,... | collective-permute-start | bytes 589832 | tf_op jit(solution)/shard_map/ppermute | solution.py:266
  37.7 2.6 %all-to-all-done.picked = bf16[4,256,256]{2,1,0:T(8,128)(2,1)} async-done(((bf16[4,256,256]{2,1,0:T(8,128)(2,1)}), bf16[4,256,256]{2,1,0:T(8,128)(2,1)}, u32[]{:S(2)}, u32[]{:S(2)}) %all-to-all-start) | async-done | bytes 524320 | tf_op jit(solution)/shard_map/all_to_all | solution.py:282
  40.4 2.0 %shard_map.119 = s16[4,272,256]{2,1,0:T(8,128)(2,1)} custom-call(bf16[4,256,256]{2,1,0:T(8,128)(2,1)} %all-to-all-done.picked), custom_call_target="tpu_custom_call" | custom-call | tf_op jit(solution)/shard_map/pallas_call | solution.py:245
  42.4 3.5 %all-to-all-start.1 = ((s16[4,272,256]{2,1,0:T(8,128)(2,1)}), s16[4,272,256]{2,1,0:T(8,128)(2,1)S(1)}, u32[]{:S(2)}, u32[]{:S(2)}) async-start(s16[4,272,256]{2,1,0:T(8,128)(2,1)} %shard_map.119), calls=%async_computation.1 | async-start | bytes 1114112 | tf_op jit(solution)/shard_map/all_to_all | solution.py:295
  45.9 3.0 %shard_map.112 = (s16[272,512]{1,0:T(8,128)(2,1)}, s16[528,512]{1,0:T(8,128)(2,1)}, s16[528,512]{1,0:T(8,128)(2,1)}) custom-call(bf16[128,2560]{1,0:T(8,128)(2,1)S(1)} %get-tuple-element.32.own, bf16[128,2560]{1,0:T(8,128)(2,1)S(1)} %collective-permute-done.near, bf16[128,1792]{1,0:T(8,128)(2,1)} %collective-permute-done.1.y_early, ...), custom_call_target="tpu_custom_call" | custom-call | tf_op jit(solution)/shard_map/pallas_call | solution.py:245
  48.9 8.4 %collective-permute-start.7 = (s16[272,512]{1,0:T(8,128)(2,1)}, s16[272,512]{1,0:T(8,128)(2,1)}, u32[]{:S(2)}, u32[]{:S(2)}) collective-permute-start(s16[272,512]{1,0:T(8,128)(2,1)} %get-tuple-element.45), channel_id=1, source_target_pairs={{0,8},{1,25},{2,10},{3,27},{4,12},{5,29},{6,14},{7,31},{8,16},{9,1... | collective-permute-start | bytes 835592 | tf_op jit(solution)/shard_map/ppermute | solution.py:266
  57.3 2.2 %collective-permute-start.8 = (s16[528,512]{1,0:T(8,128)(2,1)}, s16[528,512]{1,0:T(8,128)(2,1)S(1)}, u32[]{:S(2)}, u32[]{:S(2)}) collective-permute-start(s16[528,512]{1,0:T(8,128)(2,1)} %get-tuple-element.50), channel_id=1, source_target_pairs={{0,4},{1,29},{2,6},{3,31},{4,8},{5,1},{6,10},{7,3},{8,12},{9,5},{1... | collective-permute-start | bytes 1622024 | tf_op jit(solution)/shard_map/ppermute | solution.py:266
  59.5 3.1 %collective-permute-start.9 = (s16[528,512]{1,0:T(8,128)(2,1)}, s16[528,512]{1,0:T(8,128)(2,1)S(1)}, u32[]{:S(2)}, u32[]{:S(2)}) collective-permute-start(s16[528,512]{1,0:T(8,128)(2,1)} %get-tuple-element.51), channel_id=1, source_target_pairs={{0,28},{1,5},{2,30},{3,7},{4,0},{5,9},{6,2},{7,11},{8,4},{9,13},{1... | collective-permute-start | bytes 1622024 | tf_op jit(solution)/shard_map/ppermute | solution.py:266
  62.6 1.6 %shard_map.116 = (f32[256,512]{1,0:T(8,128)S(1)}, f32[256,512]{1,0:T(8,128)S(1)}) custom-call(bf16[128,2560]{1,0:T(8,128)(2,1)S(1)} %get-tuple-element.32.own, bf16[128,2560]{1,0:T(8,128)(2,1)S(1)} %collective-permute-done.near, bf16[128,1792]{1,0:T(8,128)(2,1)} %collective-permute-done.1.y_early, bf16[128,1792]{1,0:T(8,128)(2,1)} %collective-permute-done.2.x_early, ...), custom_call_target="tpu_custom_call" | custom-call | flops 14000000000 | tf_op jit(solution)/shard_map/pallas_call | solution.py:245
  68.5 2.6 %shard_map.113 = (f32[256,512]{1,0:T(8,128)S(1)}, f32[256,512]{1,0:T(8,128)S(1)}, f32[256,512]{1,0:T(8,128)S(1)}) custom-call(bf16[128,2560]{1,0:T(8,128)(2,1)S(1)} %get-tuple-element.32.own, bf16[128,2560]{1,0:T(8,128)(2,1)S(1)} %collective-permute-done.near, bf16[128,1792]{1,0:T(8,128)(2,1)} %collective-permute-done.1.y_early, ...), custom_call_target="tpu_custom_call" | custom-call | tf_op jit(solution)/shard_map/pallas_call | solution.py:245
  71.1 2.3 %collective-permute-start.5 = (f32[256,512]{1,0:T(8,128)S(1)}, f32[256,512]{1,0:T(8,128)S(1)}, u32[]{:S(2)}, u32[]{:S(2)}) collective-permute-start(f32[256,512]{1,0:T(8,128)S(1)} %get-tuple-element.41), channel_id=1, source_target_pairs={{0,1},{1,0},{2,3},{3,2},{4,5},{5,4},{6,7},{7,6},{8,9},{9,8},{10,11... | collective-permute-start | bytes 1572872 | tf_op jit(solution)/shard_map/ppermute | solution.py:266
  73.4 2.6 %collective-permute-done.8.ahead = s16[528,512]{1,0:T(8,128)(2,1)S(1)} collective-permute-done((s16[528,512]{1,0:T(8,128)(2,1)}, s16[528,512]{1,0:T(8,128)(2,1)S(1)}, u32[]{:S(2)}, u32[]{:S(2)}) %collective-permute-start.8) | collective-permute-done | bytes 540704 | tf_op jit(solution)/shard_map/ppermute | solution.py:266
  77.1 2.0 %shard_map.117 = (s16[272,512]{1,0:T(8,128)(2,1)}, s16[272,512]{1,0:T(8,128)(2,1)}) custom-call(f32[256,512]{1,0:T(8,128)S(1)} %copy-done.12, f32[256,512]{1,0:T(8,128)S(1)} %copy-done.14, s16[272,512]{1,0:T(8,128)(2,1)} %collective-permute-done.7.far, s16[528,512]{1,0:T(8,128)(2,1)S(1)} %collective-permute-done.8.ahead, ...), custom_call_target="tpu_custom_call" | custom-call | flops 12000000000 | tf_op jit(solution)/shard_map/pallas_call | solution.py:245
  79.2 2.6 %collective-permute-start.10 = (s16[272,512]{1,0:T(8,128)(2,1)}, s16[272,512]{1,0:T(8,128)(2,1)S(1)}, u32[]{:S(2)}, u32[]{:S(2)}) collective-permute-start(s16[272,512]{1,0:T(8,128)(2,1)} %get-tuple-element.52), channel_id=1, source_target_pairs={{0,8},{1,25},{2,10},{3,27},{4,12},{5,29},{6,14},{7,31},{8,16},{9,1... | collective-permute-start | bytes 835592 | tf_op jit(solution)/shard_map/ppermute | solution.py:266
  81.8 3.7 %collective-permute-start.11 = (s16[272,512]{1,0:T(8,128)(2,1)}, s16[272,512]{1,0:T(8,128)(2,1)S(1)}, u32[]{:S(2)}, u32[]{:S(2)}) collective-permute-start(s16[272,512]{1,0:T(8,128)(2,1)} %get-tuple-element.53), channel_id=1, source_target_pairs={{0,24},{1,9},{2,26},{3,11},{4,28},{5,13},{6,30},{7,15},{8,0},{9,17... | collective-permute-start | bytes 835592 | tf_op jit(solution)/shard_map/ppermute | solution.py:266
  86.3 2.3 %collective-permute-start.6 = (f32[128,512]{1,0:T(8,128)}, f32[128,512]{1,0:T(8,128)S(1)}, u32[]{:S(2)}, u32[]{:S(2)}) collective-permute-start(f32[128,512]{1,0:T(8,128)} %get-tuple-element.43), channel_id=1, source_target_pairs={{0,2},{1,3},{2,0},{3,1},{4,6},{5,7},{6,4},{7,5},{8,10},{9,11},{10,... | collective-permute-start | bytes 786440 | tf_op jit(solution)/shard_map/ppermute | solution.py:266
  91.5 7.7 %collective-permute-done.11.behind2 = s16[272,512]{1,0:T(8,128)(2,1)S(1)} collective-permute-done((s16[272,512]{1,0:T(8,128)(2,1)}, s16[272,512]{1,0:T(8,128)(2,1)S(1)}, u32[]{:S(2)}, u32[]{:S(2)}) %collective-permute-start.11) | collective-permute-done | bytes 278560 | tf_op jit(solution)/shard_map/ppermute | solution.py:266
  99.2 1.8 %shard_map.121 = (f32[256,512]{1,0:T(8,128)}, bf16[256,512]{1,0:T(8,128)(2,1)}) custom-call(s32[4]{0:T(128)S(1)} %copy-done.10, f32[256,512]{1,0:T(8,128)S(1)} %copy-done.7, s16[272,512]{1,0:T(8,128)(2,1)S(1)} %collective-permute-done.10.ahead2, s16[272,512]{1,0:T(8,128)(2,1)S(1)} %collective-permute-done.11.behind2, ...), custom_call_target="tpu_custom_call" | custom-call | tf_op jit(solution)/shard_map/pallas_call | solution.py:245
  (49 shorter events, 13.2 us)
Async XLA Ops:
  7.2 18.0 %copy-start.1 = (bf16[1,256,512]{2,1,0:T(8,128)(2,1)S(1)}, bf16[1,256,512]{2,1,0:T(8,128)(2,1)}, u32[]{:S(2)}) copy-start(bf16[1,256,512]{2,1,0:T(8,128)(2,1)} %param.9) | copy-start | bytes 786436
  7.2 18.0 %copy-start.10 = (s32[4]{0:T(128)S(1)}, s32[4]{0:T(128)}, u32[]{:S(2)}) copy-start(s32[4]{0:T(128)} %frag.3) | copy-start | bytes 52
  7.2 58.6 %all-gather.3.cloned.1.call-start = ((), (), s32[]{:S(2)}) async-start(), calls=%async_computation.2 | async-start | bytes 2359296 | tf_op jit(solution)/shard_map/all_gather | solution.py:264
  7.9 23.0 %copy-start = (bf16[1,128,8192]{2,1,0:T(8,128)(2,1)S(1)}, bf16[1,128,8192]{2,1,0:T(8,128)(2,1)}, u32[]{:S(2)}) copy-start(bf16[1,128,8192]{2,1,0:T(8,128)(2,1)} %param.7) | copy-start | bytes 6291460
  7.9 23.0 %copy-start.5 = (bf16[1,128,512]{2,1,0:T(8,128)(2,1)S(1)}, bf16[1,128,512]{2,1,0:T(8,128)(2,1)}, u32[]{:S(2)}) copy-start(bf16[1,128,512]{2,1,0:T(8,128)(2,1)} %param.8) | copy-start | bytes 393220
  10.9 35.0 %collective-permute-start = (bf16[128,2560]{1,0:T(8,128)(2,1)}, bf16[128,2560]{1,0:T(8,128)(2,1)S(1)}, u32[]{:S(2)}, u32[]{:S(2)}) collective-permute-start(bf16[128,2560]{1,0:T(8,128)(2,1)} %get-tuple-element.33), channel_id=1, source_target_pairs={{0,1},{1,0},{2,3},{3,2},{4,5},{5,4},{6,7},{7,6},{8,9},{9,8},{10,11... | collective-permute-start | bytes 1966088 | tf_op jit(solution)/shard_map/ppermute | solution.py:266
  19.7 26.1 %collective-permute-start.1 = (bf16[128,1792]{1,0:T(8,128)(2,1)}, bf16[128,1792]{1,0:T(8,128)(2,1)}, u32[]{:S(2)}, u32[]{:S(2)}) collective-permute-start(bf16[128,1792]{1,0:T(8,128)(2,1)} %get-tuple-element.34), channel_id=1, source_target_pairs={{0,2},{1,3},{2,0},{3,1},{4,6},{5,7},{6,4},{7,5},{8,10},{9,11},{10,... | collective-permute-start | bytes 1376264 | tf_op jit(solution)/shard_map/ppermute | solution.py:266
  21.6 24.2 %collective-permute-start.2 = (bf16[128,1792]{1,0:T(8,128)(2,1)}, bf16[128,1792]{1,0:T(8,128)(2,1)}, u32[]{:S(2)}, u32[]{:S(2)}) collective-permute-start(bf16[128,1792]{1,0:T(8,128)(2,1)} %get-tuple-element.35), channel_id=1, source_target_pairs={{0,3},{1,2},{2,1},{3,0},{4,7},{5,6},{6,5},{7,4},{8,11},{9,10},{10,... | collective-permute-start | bytes 1376264 | tf_op jit(solution)/shard_map/ppermute | solution.py:266
  26.7 13.6 %all-to-all-start = ((bf16[4,256,256]{2,1,0:T(8,128)(2,1)}), bf16[4,256,256]{2,1,0:T(8,128)(2,1)}, u32[]{:S(2)}, u32[]{:S(2)}) async-start(bf16[4,256,256]{2,1,0:T(8,128)(2,1)} %shard_map.118), calls=%async_computation | async-start | bytes 1048576 | tf_op jit(solution)/shard_map/all_to_all | solution.py:282
  32.1 16.8 %collective-permute-start.3 = (bf16[128,768]{1,0:T(8,128)(2,1)}, bf16[128,768]{1,0:T(8,128)(2,1)S(1)}, u32[]{:S(2)}, u32[]{:S(2)}) collective-permute-start(bf16[128,768]{1,0:T(8,128)(2,1)} %get-tuple-element.37), channel_id=1, source_target_pairs={{0,2},{1,3},{2,0},{3,1},{4,6},{5,7},{6,4},{7,5},{8,10},{9,11},{10,... | collective-permute-start | bytes 589832 | tf_op jit(solution)/shard_map/ppermute | solution.py:266
  34.0 28.6 %collective-permute-start.4 = (bf16[128,768]{1,0:T(8,128)(2,1)}, bf16[128,768]{1,0:T(8,128)(2,1)S(1)}, u32[]{:S(2)}, u32[]{:S(2)}) collective-permute-start(bf16[128,768]{1,0:T(8,128)(2,1)} %get-tuple-element.39), channel_id=1, source_target_pairs={{0,3},{1,2},{2,1},{3,0},{4,7},{5,6},{6,5},{7,4},{8,11},{9,10},{10,... | collective-permute-start | bytes 589832 | tf_op jit(solution)/shard_map/ppermute | solution.py:266
  42.4 46.3 %all-to-all-start.1 = ((s16[4,272,256]{2,1,0:T(8,128)(2,1)}), s16[4,272,256]{2,1,0:T(8,128)(2,1)S(1)}, u32[]{:S(2)}, u32[]{:S(2)}) async-start(s16[4,272,256]{2,1,0:T(8,128)(2,1)} %shard_map.119), calls=%async_computation.1 | async-start | bytes 1114112 | tf_op jit(solution)/shard_map/all_to_all | solution.py:295
  48.9 22.2 %collective-permute-start.7 = (s16[272,512]{1,0:T(8,128)(2,1)}, s16[272,512]{1,0:T(8,128)(2,1)}, u32[]{:S(2)}, u32[]{:S(2)}) collective-permute-start(s16[272,512]{1,0:T(8,128)(2,1)} %get-tuple-element.45), channel_id=1, source_target_pairs={{0,8},{1,25},{2,10},{3,27},{4,12},{5,29},{6,14},{7,31},{8,16},{9,1... | collective-permute-start | bytes 835592 | tf_op jit(solution)/shard_map/ppermute | solution.py:266
  57.3 18.7 %collective-permute-start.8 = (s16[528,512]{1,0:T(8,128)(2,1)}, s16[528,512]{1,0:T(8,128)(2,1)S(1)}, u32[]{:S(2)}, u32[]{:S(2)}) collective-permute-start(s16[528,512]{1,0:T(8,128)(2,1)} %get-tuple-element.50), channel_id=1, source_target_pairs={{0,4},{1,29},{2,6},{3,31},{4,8},{5,1},{6,10},{7,3},{8,12},{9,5},{1... | collective-permute-start | bytes 1622024 | tf_op jit(solution)/shard_map/ppermute | solution.py:266
  59.5 17.7 %collective-permute-start.9 = (s16[528,512]{1,0:T(8,128)(2,1)}, s16[528,512]{1,0:T(8,128)(2,1)S(1)}, u32[]{:S(2)}, u32[]{:S(2)}) collective-permute-start(s16[528,512]{1,0:T(8,128)(2,1)} %get-tuple-element.51), channel_id=1, source_target_pairs={{0,28},{1,5},{2,30},{3,7},{4,0},{5,9},{6,2},{7,11},{8,4},{9,13},{1... | collective-permute-start | bytes 1622024 | tf_op jit(solution)/shard_map/ppermute | solution.py:266
  68.5 8.7 %copy-start.12 = (f32[256,512]{1,0:T(8,128)S(1)}, f32[256,512]{1,0:T(8,128)}, u32[]{:S(2)}) copy-start(f32[256,512]{1,0:T(8,128)} %copy-done.11) | copy-start | bytes 1572868
  68.5 8.7 %copy-start.14 = (f32[256,512]{1,0:T(8,128)S(1)}, f32[256,512]{1,0:T(8,128)}, u32[]{:S(2)}) copy-start(f32[256,512]{1,0:T(8,128)} %copy-done.13) | copy-start | bytes 1572868
  71.1 8.1 %copy-start.6 = (f32[256,512]{1,0:T(8,128)}, f32[256,512]{1,0:T(8,128)S(1)}, u32[]{:S(2)}) copy-start(f32[256,512]{1,0:T(8,128)S(1)} %get-tuple-element.46.base) | copy-start | bytes 1572868
  71.1 14.4 %collective-permute-start.5 = (f32[256,512]{1,0:T(8,128)S(1)}, f32[256,512]{1,0:T(8,128)S(1)}, u32[]{:S(2)}, u32[]{:S(2)}) collective-permute-start(f32[256,512]{1,0:T(8,128)S(1)} %get-tuple-element.41), channel_id=1, source_target_pairs={{0,1},{1,0},{2,3},{3,2},{4,5},{5,4},{6,7},{7,6},{8,9},{9,8},{10,11... | collective-permute-start | bytes 1572872 | tf_op jit(solution)/shard_map/ppermute | solution.py:266
  79.2 20.1 %copy-start.2 = (bf16[1,256,512]{2,1,0:T(8,128)(2,1)S(1)}, bf16[1,256,512]{2,1,0:T(8,128)(2,1)}, u32[]{:S(2)}) copy-start(bf16[1,256,512]{2,1,0:T(8,128)(2,1)} %param.9) | copy-start | bytes 786436
  79.2 20.1 %copy-start.7 = (f32[256,512]{1,0:T(8,128)S(1)}, f32[256,512]{1,0:T(8,128)}, u32[]{:S(2)}) copy-start(f32[256,512]{1,0:T(8,128)} %copy-done.6) | copy-start | bytes 1572868
  79.2 12.3 %collective-permute-start.10 = (s16[272,512]{1,0:T(8,128)(2,1)}, s16[272,512]{1,0:T(8,128)(2,1)S(1)}, u32[]{:S(2)}, u32[]{:S(2)}) collective-permute-start(s16[272,512]{1,0:T(8,128)(2,1)} %get-tuple-element.52), channel_id=1, source_target_pairs={{0,8},{1,25},{2,10},{3,27},{4,12},{5,29},{6,14},{7,31},{8,16},{9,1... | collective-permute-start | bytes 835592 | tf_op jit(solution)/shard_map/ppermute | solution.py:266
  81.8 17.4 %collective-permute-start.11 = (s16[272,512]{1,0:T(8,128)(2,1)}, s16[272,512]{1,0:T(8,128)(2,1)S(1)}, u32[]{:S(2)}, u32[]{:S(2)}) collective-permute-start(s16[272,512]{1,0:T(8,128)(2,1)} %get-tuple-element.53), channel_id=1, source_target_pairs={{0,24},{1,9},{2,26},{3,11},{4,28},{5,13},{6,30},{7,15},{8,0},{9,17... | collective-permute-start | bytes 835592 | tf_op jit(solution)/shard_map/ppermute | solution.py:266
  86.3 14.7 %collective-permute-start.6 = (f32[128,512]{1,0:T(8,128)}, f32[128,512]{1,0:T(8,128)S(1)}, u32[]{:S(2)}, u32[]{:S(2)}) collective-permute-start(f32[128,512]{1,0:T(8,128)} %get-tuple-element.43), channel_id=1, source_target_pairs={{0,2},{1,3},{2,0},{3,1},{4,6},{5,7},{6,4},{7,5},{8,10},{9,11},{10,... | collective-permute-start | bytes 786440 | tf_op jit(solution)/shard_map/ppermute | solution.py:266
  (6 other events, 6.1 us)
Sparse Core Ops, SparseCore 0:
  10.1 46.4 all-gather.2

commit v5 on v4

--- a/solution.py
+++ b/solution.py
@@ -238,12 +238,15 @@
     out[...] = ((mine[...] + got[...]) * (D ** -0.5)).astype(BF16)
 
 
-def call(kernel, outs, *args, scalars=0, copies=0, hint=0, first=False):
+def call(kernel, outs, *args, scalars=0, copies=0, hint=0, first=False, narrow=0):
     space = pl.ANY if copies else pltpu.VMEM
     specs = [pl.BlockSpec(memory_space=pltpu.SMEM)] * scalars
     specs += [pl.BlockSpec(memory_space=space)] * (len(args) - scalars)
+    for n in range(narrow):
+        specs[n] = pl.BlockSpec((TOK, SPLIT), lambda i: (0, 0))
     return pl.pallas_call(
         kernel,
+        grid=(1,) if narrow else (),
         out_shape=list(outs),
         in_specs=specs,
         out_specs=[pl.BlockSpec(memory_space=pltpu.VMEM)] * len(outs),
@@ -284,7 +287,7 @@
     one = shape(CODED, width, kind=jnp.int16)
     two = shape(2 * ROWS + GROUP, width, kind=jnp.int16)
     wide = shape(ROWS, width, kind=F32)
-    far, ahead, behind = call(early_kernel, [one, two, two], own, near, y_early, x_early)
+    far, ahead, behind = call(early_kernel, [one, two, two], own, near, y_early, x_early, narrow=2)
     far, y_late = lax.optimization_barrier((far, y_late))
     far = send(far, ring(2))
     ahead = send(ahead, ring(1))

time: 109 us -> 109 us (level)
  no operation moved by 1% of the time
where the time goes in v5:
time: 109 us
  starting transfers between devices  52.2 us (48%)
  Pallas kernels  21.2 us (19%)
  waiting for transfers between devices  14.8 us (14%)
  between operations  14.3 us (13%)
  local copies, waits for them, and re-layouts  6.15 us (6%)
    ppermute x12, starting transfers between devices, shards(): send = lambda x, pairs: lax.ppermute(x, 'fsdp', pairs)  44.5 us
    pallas_call x12, Pallas kernels, call(): pl.pallas_call(kernel, grid=(1,) if narrow else (), out_shape=list(outs),...  21.2 us
    ppermute x12, waiting for transfers between devices, shards(): send = lambda x, pairs: lax.ppermute(x, 'fsdp', pairs)  11.5 us
    unnamed x30, local copies, waits for them, and re-layouts  6.15 us
    all_to_all x1, starting transfers between devices, shards(): picked = lax.all_to_all(picked, 'rep', 0, 0, axis_index_groups=x_groups())  4.17 us
    all_to_all x1, starting transfers between devices, shards(): sums = lax.all_to_all(sums, 'rep', 0, 0, axis_index_groups=y_groups())  3.47 us
    all_to_all x1, waiting for transfers between devices, shards(): picked = lax.all_to_all(picked, 'rep', 0, 0, axis_index_groups=x_groups())  2.63 us
  transfers between devices with their start and end apart: 15, of which 4 were waited for; matrix products, arithmetic and copies ran while one was open for 0% of the time, Pallas kernels for 19%

profile of v5, /device:TPU:1, one launch (start us, length us, event | category | flops | bytes accessed | tf_op | source)
XLA Modules:
  0.0 108.6 jit_solution(10491597224622173722)
XLA Ops:
  7.9 3.0 %shard_map.111 = (bf16[128,1792]{1,0:T(8,128)(2,1)}, bf16[128,1792]{1,0:T(8,128)(2,1)}, bf16[128,2560]{1,0:T(8,128)(2,1)}) custom-call(bf16[128,8192]{1,0:T(8,128)(2,1)} %bitcast.8, bf16[128,512]{1,0:T(8,128)(2,1)} %bitcast.14), custom_call_target="tpu_custom_call" | custom-call | tf_op jit(solution)/shard_map/pallas_call | solution.py:247
  10.9 8.8 %collective-permute-start = (bf16[128,2560]{1,0:T(8,128)(2,1)}, bf16[128,2560]{1,0:T(8,128)(2,1)S(1)}, u32[]{:S(2)}, u32[]{:S(2)}) collective-permute-start(bf16[128,2560]{1,0:T(8,128)(2,1)} %get-tuple-element.33), channel_id=1, source_target_pairs={{0,1},{1,0},{2,3},{3,2},{4,5},{5,4},{6,7},{7,6},{8,9},{9,8},{10,11... | collective-permute-start | bytes 1966088 | tf_op jit(solution)/shard_map/ppermute | solution.py:269
  19.7 1.9 %collective-permute-start.1 = (bf16[128,1792]{1,0:T(8,128)(2,1)}, bf16[128,1792]{1,0:T(8,128)(2,1)}, u32[]{:S(2)}, u32[]{:S(2)}) collective-permute-start(bf16[128,1792]{1,0:T(8,128)(2,1)} %get-tuple-element.34), channel_id=1, source_target_pairs={{0,2},{1,3},{2,0},{3,1},{4,6},{5,7},{6,4},{7,5},{8,10},{9,11},{10,... | collective-permute-start | bytes 1376264 | tf_op jit(solution)/shard_map/ppermute | solution.py:269
  21.6 3.5 %collective-permute-start.2 = (bf16[128,1792]{1,0:T(8,128)(2,1)}, bf16[128,1792]{1,0:T(8,128)(2,1)}, u32[]{:S(2)}, u32[]{:S(2)}) collective-permute-start(bf16[128,1792]{1,0:T(8,128)(2,1)} %get-tuple-element.35), channel_id=1, source_target_pairs={{0,3},{1,2},{2,1},{3,0},{4,7},{5,6},{6,5},{7,4},{8,11},{9,10},{10,... | collective-permute-start | bytes 1376264 | tf_op jit(solution)/shard_map/ppermute | solution.py:269
  26.7 4.2 %all-to-all-start = ((bf16[4,256,256]{2,1,0:T(8,128)(2,1)}), bf16[4,256,256]{2,1,0:T(8,128)(2,1)}, u32[]{:S(2)}, u32[]{:S(2)}) async-start(bf16[4,256,256]{2,1,0:T(8,128)(2,1)} %shard_map.118), calls=%async_computation | async-start | bytes 1048576 | tf_op jit(solution)/shard_map/all_to_all | solution.py:285
  32.1 1.9 %collective-permute-start.3 = (bf16[128,768]{1,0:T(8,128)(2,1)}, bf16[128,768]{1,0:T(8,128)(2,1)S(1)}, u32[]{:S(2)}, u32[]{:S(2)}) collective-permute-start(bf16[128,768]{1,0:T(8,128)(2,1)} %get-tuple-element.37), channel_id=1, source_target_pairs={{0,2},{1,3},{2,0},{3,1},{4,6},{5,7},{6,4},{7,5},{8,10},{9,11},{10,... | collective-permute-start | bytes 589832 | tf_op jit(solution)/shard_map/ppermute | solution.py:269
  34.0 3.7 %collective-permute-start.4 = (bf16[128,768]{1,0:T(8,128)(2,1)}, bf16[128,768]{1,0:T(8,128)(2,1)S(1)}, u32[]{:S(2)}, u32[]{:S(2)}) collective-permute-start(bf16[128,768]{1,0:T(8,128)(2,1)} %get-tuple-element.39), channel_id=1, source_target_pairs={{0,3},{1,2},{2,1},{3,0},{4,7},{5,6},{6,5},{7,4},{8,11},{9,10},{10,... | collective-permute-start | bytes 589832 | tf_op jit(solution)/shard_map/ppermute | solution.py:269
  37.7 2.6 %all-to-all-done.picked = bf16[4,256,256]{2,1,0:T(8,128)(2,1)} async-done(((bf16[4,256,256]{2,1,0:T(8,128)(2,1)}), bf16[4,256,256]{2,1,0:T(8,128)(2,1)}, u32[]{:S(2)}, u32[]{:S(2)}) %all-to-all-start) | async-done | bytes 524320 | tf_op jit(solution)/shard_map/all_to_all | solution.py:285
  40.4 2.0 %shard_map.119 = s16[4,272,256]{2,1,0:T(8,128)(2,1)} custom-call(bf16[4,256,256]{2,1,0:T(8,128)(2,1)} %all-to-all-done.picked), custom_call_target="tpu_custom_call" | custom-call | tf_op jit(solution)/shard_map/pallas_call | solution.py:247
  42.4 3.5 %all-to-all-start.1 = ((s16[4,272,256]{2,1,0:T(8,128)(2,1)}), s16[4,272,256]{2,1,0:T(8,128)(2,1)S(1)}, u32[]{:S(2)}, u32[]{:S(2)}) async-start(s16[4,272,256]{2,1,0:T(8,128)(2,1)} %shard_map.119), calls=%async_computation.1 | async-start | bytes 1114112 | tf_op jit(solution)/shard_map/all_to_all | solution.py:298
  45.9 3.1 %shard_map.112 = (s16[272,512]{1,0:T(8,128)(2,1)}, s16[528,512]{1,0:T(8,128)(2,1)}, s16[528,512]{1,0:T(8,128)(2,1)}) custom-call(bf16[128,2560]{1,0:T(8,128)(2,1)S(1)} %get-tuple-element.32.own, bf16[128,2560]{1,0:T(8,128)(2,1)S(1)} %collective-permute-done.near, bf16[128,1792]{1,0:T(8,128)(2,1)} %collective-permute-done.1.y_early, ...), custom_call_target="tpu_custom_call" | custom-call | tf_op jit(solution)/shard_map/pallas_call | solution.py:247
  49.0 8.4 %collective-permute-start.7 = (s16[272,512]{1,0:T(8,128)(2,1)}, s16[272,512]{1,0:T(8,128)(2,1)}, u32[]{:S(2)}, u32[]{:S(2)}) collective-permute-start(s16[272,512]{1,0:T(8,128)(2,1)} %get-tuple-element.45), channel_id=1, source_target_pairs={{0,8},{1,25},{2,10},{3,27},{4,12},{5,29},{6,14},{7,31},{8,16},{9,1... | collective-permute-start | bytes 835592 | tf_op jit(solution)/shard_map/ppermute | solution.py:269
  57.4 2.2 %collective-permute-start.8 = (s16[528,512]{1,0:T(8,128)(2,1)}, s16[528,512]{1,0:T(8,128)(2,1)S(1)}, u32[]{:S(2)}, u32[]{:S(2)}) collective-permute-start(s16[528,512]{1,0:T(8,128)(2,1)} %get-tuple-element.50), channel_id=1, source_target_pairs={{0,4},{1,29},{2,6},{3,31},{4,8},{5,1},{6,10},{7,3},{8,12},{9,5},{1... | collective-permute-start | bytes 1622024 | tf_op jit(solution)/shard_map/ppermute | solution.py:269
  59.5 3.1 %collective-permute-start.9 = (s16[528,512]{1,0:T(8,128)(2,1)}, s16[528,512]{1,0:T(8,128)(2,1)S(1)}, u32[]{:S(2)}, u32[]{:S(2)}) collective-permute-start(s16[528,512]{1,0:T(8,128)(2,1)} %get-tuple-element.51), channel_id=1, source_target_pairs={{0,28},{1,5},{2,30},{3,7},{4,0},{5,9},{6,2},{7,11},{8,4},{9,13},{1... | collective-permute-start | bytes 1622024 | tf_op jit(solution)/shard_map/ppermute | solution.py:269
  62.7 1.6 %shard_map.116 = (f32[256,512]{1,0:T(8,128)S(1)}, f32[256,512]{1,0:T(8,128)S(1)}) custom-call(bf16[128,2560]{1,0:T(8,128)(2,1)S(1)} %get-tuple-element.32.own, bf16[128,2560]{1,0:T(8,128)(2,1)S(1)} %collective-permute-done.near, bf16[128,1792]{1,0:T(8,128)(2,1)} %collective-permute-done.1.y_early, bf16[128,1792]{1,0:T(8,128)(2,1)} %collective-permute-done.2.x_early, ...), custom_call_target="tpu_custom_call" | custom-call | flops 14000000000 | tf_op jit(solution)/shard_map/pallas_call | solution.py:247
  68.5 2.6 %shard_map.113 = (f32[256,512]{1,0:T(8,128)S(1)}, f32[256,512]{1,0:T(8,128)S(1)}, f32[256,512]{1,0:T(8,128)S(1)}) custom-call(bf16[128,2560]{1,0:T(8,128)(2,1)S(1)} %get-tuple-element.32.own, bf16[128,2560]{1,0:T(8,128)(2,1)S(1)} %collective-permute-done.near, bf16[128,1792]{1,0:T(8,128)(2,1)} %collective-permute-done.1.y_early, ...), custom_call_target="tpu_custom_call" | custom-call | tf_op jit(solution)/shard_map/pallas_call | solution.py:247
  71.2 2.3 %collective-permute-start.5 = (f32[256,512]{1,0:T(8,128)S(1)}, f32[256,512]{1,0:T(8,128)S(1)}, u32[]{:S(2)}, u32[]{:S(2)}) collective-permute-start(f32[256,512]{1,0:T(8,128)S(1)} %get-tuple-element.41), channel_id=1, source_target_pairs={{0,1},{1,0},{2,3},{3,2},{4,5},{5,4},{6,7},{7,6},{8,9},{9,8},{10,11... | collective-permute-start | bytes 1572872 | tf_op jit(solution)/shard_map/ppermute | solution.py:269
  73.5 2.5 %collective-permute-done.8.ahead = s16[528,512]{1,0:T(8,128)(2,1)S(1)} collective-permute-done((s16[528,512]{1,0:T(8,128)(2,1)}, s16[528,512]{1,0:T(8,128)(2,1)S(1)}, u32[]{:S(2)}, u32[]{:S(2)}) %collective-permute-start.8) | collective-permute-done | bytes 540704 | tf_op jit(solution)/shard_map/ppermute | solution.py:269
  77.2 2.0 %shard_map.117 = (s16[272,512]{1,0:T(8,128)(2,1)}, s16[272,512]{1,0:T(8,128)(2,1)}) custom-call(f32[256,512]{1,0:T(8,128)S(1)} %copy-done.12, f32[256,512]{1,0:T(8,128)S(1)} %copy-done.14, s16[272,512]{1,0:T(8,128)(2,1)} %collective-permute-done.7.far, s16[528,512]{1,0:T(8,128)(2,1)S(1)} %collective-permute-done.8.ahead, ...), custom_call_target="tpu_custom_call" | custom-call | flops 12000000000 | tf_op jit(solution)/shard_map/pallas_call | solution.py:247
  79.3 2.6 %collective-permute-start.10 = (s16[272,512]{1,0:T(8,128)(2,1)}, s16[272,512]{1,0:T(8,128)(2,1)S(1)}, u32[]{:S(2)}, u32[]{:S(2)}) collective-permute-start(s16[272,512]{1,0:T(8,128)(2,1)} %get-tuple-element.52), channel_id=1, source_target_pairs={{0,8},{1,25},{2,10},{3,27},{4,12},{5,29},{6,14},{7,31},{8,16},{9,1... | collective-permute-start | bytes 835592 | tf_op jit(solution)/shard_map/ppermute | solution.py:269
  81.9 3.7 %collective-permute-start.11 = (s16[272,512]{1,0:T(8,128)(2,1)}, s16[272,512]{1,0:T(8,128)(2,1)S(1)}, u32[]{:S(2)}, u32[]{:S(2)}) collective-permute-start(s16[272,512]{1,0:T(8,128)(2,1)} %get-tuple-element.53), channel_id=1, source_target_pairs={{0,24},{1,9},{2,26},{3,11},{4,28},{5,13},{6,30},{7,15},{8,0},{9,17... | collective-permute-start | bytes 835592 | tf_op jit(solution)/shard_map/ppermute | solution.py:269
  86.4 2.3 %collective-permute-start.6 = (f32[128,512]{1,0:T(8,128)}, f32[128,512]{1,0:T(8,128)S(1)}, u32[]{:S(2)}, u32[]{:S(2)}) collective-permute-start(f32[128,512]{1,0:T(8,128)} %get-tuple-element.43), channel_id=1, source_target_pairs={{0,2},{1,3},{2,0},{3,1},{4,6},{5,7},{6,4},{7,5},{8,10},{9,11},{10,... | collective-permute-start | bytes 786440 | tf_op jit(solution)/shard_map/ppermute | solution.py:269
  91.6 7.7 %collective-permute-done.11.behind2 = s16[272,512]{1,0:T(8,128)(2,1)S(1)} collective-permute-done((s16[272,512]{1,0:T(8,128)(2,1)}, s16[272,512]{1,0:T(8,128)(2,1)S(1)}, u32[]{:S(2)}, u32[]{:S(2)}) %collective-permute-start.11) | collective-permute-done | bytes 278560 | tf_op jit(solution)/shard_map/ppermute | solution.py:269
  99.3 1.8 %shard_map.121 = (f32[256,512]{1,0:T(8,128)}, bf16[256,512]{1,0:T(8,128)(2,1)}) custom-call(s32[4]{0:T(128)S(1)} %copy-done.10, f32[256,512]{1,0:T(8,128)S(1)} %copy-done.7, s16[272,512]{1,0:T(8,128)(2,1)S(1)} %collective-permute-done.10.ahead2, s16[272,512]{1,0:T(8,128)(2,1)S(1)} %collective-permute-done.11.behind2, ...), custom_call_target="tpu_custom_call" | custom-call | tf_op jit(solution)/shard_map/pallas_call | solution.py:247
  (49 shorter events, 13.2 us)
Async XLA Ops:
  7.2 18.0 %copy-start.1 = (bf16[1,256,512]{2,1,0:T(8,128)(2,1)S(1)}, bf16[1,256,512]{2,1,0:T(8,128)(2,1)}, u32[]{:S(2)}) copy-start(bf16[1,256,512]{2,1,0:T(8,128)(2,1)} %param.9) | copy-start | bytes 786436
  7.2 18.0 %copy-start.10 = (s32[4]{0:T(128)S(1)}, s32[4]{0:T(128)}, u32[]{:S(2)}) copy-start(s32[4]{0:T(128)} %frag.3) | copy-start | bytes 52
  7.2 58.7 %all-gather.3.cloned.1.call-start = ((), (), s32[]{:S(2)}) async-start(), calls=%async_computation.2 | async-start | bytes 2359296 | tf_op jit(solution)/shard_map/all_gather | solution.py:267
  7.9 23.0 %copy-start = (bf16[1,128,8192]{2,1,0:T(8,128)(2,1)S(1)}, bf16[1,128,8192]{2,1,0:T(8,128)(2,1)}, u32[]{:S(2)}) copy-start(bf16[1,128,8192]{2,1,0:T(8,128)(2,1)} %param.7) | copy-start | bytes 6291460
  7.9 23.0 %copy-start.5 = (bf16[1,128,512]{2,1,0:T(8,128)(2,1)S(1)}, bf16[1,128,512]{2,1,0:T(8,128)(2,1)}, u32[]{:S(2)}) copy-start(bf16[1,128,512]{2,1,0:T(8,128)(2,1)} %param.8) | copy-start | bytes 393220
  10.9 35.0 %collective-permute-start = (bf16[128,2560]{1,0:T(8,128)(2,1)}, bf16[128,2560]{1,0:T(8,128)(2,1)S(1)}, u32[]{:S(2)}, u32[]{:S(2)}) collective-permute-start(bf16[128,2560]{1,0:T(8,128)(2,1)} %get-tuple-element.33), channel_id=1, source_target_pairs={{0,1},{1,0},{2,3},{3,2},{4,5},{5,4},{6,7},{7,6},{8,9},{9,8},{10,11... | collective-permute-start | bytes 1966088 | tf_op jit(solution)/shard_map/ppermute | solution.py:269
  19.7 26.1 %collective-permute-start.1 = (bf16[128,1792]{1,0:T(8,128)(2,1)}, bf16[128,1792]{1,0:T(8,128)(2,1)}, u32[]{:S(2)}, u32[]{:S(2)}) collective-permute-start(bf16[128,1792]{1,0:T(8,128)(2,1)} %get-tuple-element.34), channel_id=1, source_target_pairs={{0,2},{1,3},{2,0},{3,1},{4,6},{5,7},{6,4},{7,5},{8,10},{9,11},{10,... | collective-permute-start | bytes 1376264 | tf_op jit(solution)/shard_map/ppermute | solution.py:269
  21.6 24.2 %collective-permute-start.2 = (bf16[128,1792]{1,0:T(8,128)(2,1)}, bf16[128,1792]{1,0:T(8,128)(2,1)}, u32[]{:S(2)}, u32[]{:S(2)}) collective-permute-start(bf16[128,1792]{1,0:T(8,128)(2,1)} %get-tuple-element.35), channel_id=1, source_target_pairs={{0,3},{1,2},{2,1},{3,0},{4,7},{5,6},{6,5},{7,4},{8,11},{9,10},{10,... | collective-permute-start | bytes 1376264 | tf_op jit(solution)/shard_map/ppermute | solution.py:269
  26.7 13.6 %all-to-all-start = ((bf16[4,256,256]{2,1,0:T(8,128)(2,1)}), bf16[4,256,256]{2,1,0:T(8,128)(2,1)}, u32[]{:S(2)}, u32[]{:S(2)}) async-start(bf16[4,256,256]{2,1,0:T(8,128)(2,1)} %shard_map.118), calls=%async_computation | async-start | bytes 1048576 | tf_op jit(solution)/shard_map/all_to_all | solution.py:285
  32.1 16.9 %collective-permute-start.3 = (bf16[128,768]{1,0:T(8,128)(2,1)}, bf16[128,768]{1,0:T(8,128)(2,1)S(1)}, u32[]{:S(2)}, u32[]{:S(2)}) collective-permute-start(bf16[128,768]{1,0:T(8,128)(2,1)} %get-tuple-element.37), channel_id=1, source_target_pairs={{0,2},{1,3},{2,0},{3,1},{4,6},{5,7},{6,4},{7,5},{8,10},{9,11},{10,... | collective-permute-start | bytes 589832 | tf_op jit(solution)/shard_map/ppermute | solution.py:269
  34.0 28.7 %collective-permute-start.4 = (bf16[128,768]{1,0:T(8,128)(2,1)}, bf16[128,768]{1,0:T(8,128)(2,1)S(1)}, u32[]{:S(2)}, u32[]{:S(2)}) collective-permute-start(bf16[128,768]{1,0:T(8,128)(2,1)} %get-tuple-element.39), channel_id=1, source_target_pairs={{0,3},{1,2},{2,1},{3,0},{4,7},{5,6},{6,5},{7,4},{8,11},{9,10},{10,... | collective-permute-start | bytes 589832 | tf_op jit(solution)/shard_map/ppermute | solution.py:269
  42.4 46.3 %all-to-all-start.1 = ((s16[4,272,256]{2,1,0:T(8,128)(2,1)}), s16[4,272,256]{2,1,0:T(8,128)(2,1)S(1)}, u32[]{:S(2)}, u32[]{:S(2)}) async-start(s16[4,272,256]{2,1,0:T(8,128)(2,1)} %shard_map.119), calls=%async_computation.1 | async-start | bytes 1114112 | tf_op jit(solution)/shard_map/all_to_all | solution.py:298
  49.0 22.2 %collective-permute-start.7 = (s16[272,512]{1,0:T(8,128)(2,1)}, s16[272,512]{1,0:T(8,128)(2,1)}, u32[]{:S(2)}, u32[]{:S(2)}) collective-permute-start(s16[272,512]{1,0:T(8,128)(2,1)} %get-tuple-element.45), channel_id=1, source_target_pairs={{0,8},{1,25},{2,10},{3,27},{4,12},{5,29},{6,14},{7,31},{8,16},{9,1... | collective-permute-start | bytes 835592 | tf_op jit(solution)/shard_map/ppermute | solution.py:269
  57.4 18.6 %collective-permute-start.8 = (s16[528,512]{1,0:T(8,128)(2,1)}, s16[528,512]{1,0:T(8,128)(2,1)S(1)}, u32[]{:S(2)}, u32[]{:S(2)}) collective-permute-start(s16[528,512]{1,0:T(8,128)(2,1)} %get-tuple-element.50), channel_id=1, source_target_pairs={{0,4},{1,29},{2,6},{3,31},{4,8},{5,1},{6,10},{7,3},{8,12},{9,5},{1... | collective-permute-start | bytes 1622024 | tf_op jit(solution)/shard_map/ppermute | solution.py:269
  59.5 17.7 %collective-permute-start.9 = (s16[528,512]{1,0:T(8,128)(2,1)}, s16[528,512]{1,0:T(8,128)(2,1)S(1)}, u32[]{:S(2)}, u32[]{:S(2)}) collective-permute-start(s16[528,512]{1,0:T(8,128)(2,1)} %get-tuple-element.51), channel_id=1, source_target_pairs={{0,28},{1,5},{2,30},{3,7},{4,0},{5,9},{6,2},{7,11},{8,4},{9,13},{1... | collective-permute-start | bytes 1622024 | tf_op jit(solution)/shard_map/ppermute | solution.py:269
  68.5 8.7 %copy-start.12 = (f32[256,512]{1,0:T(8,128)S(1)}, f32[256,512]{1,0:T(8,128)}, u32[]{:S(2)}) copy-start(f32[256,512]{1,0:T(8,128)} %copy-done.11) | copy-start | bytes 1572868
  68.5 8.7 %copy-start.14 = (f32[256,512]{1,0:T(8,128)S(1)}, f32[256,512]{1,0:T(8,128)}, u32[]{:S(2)}) copy-start(f32[256,512]{1,0:T(8,128)} %copy-done.13) | copy-start | bytes 1572868
  71.2 8.1 %copy-start.6 = (f32[256,512]{1,0:T(8,128)}, f32[256,512]{1,0:T(8,128)S(1)}, u32[]{:S(2)}) copy-start(f32[256,512]{1,0:T(8,128)S(1)} %get-tuple-element.46.base) | copy-start | bytes 1572868
  71.2 14.4 %collective-permute-start.5 = (f32[256,512]{1,0:T(8,128)S(1)}, f32[256,512]{1,0:T(8,128)S(1)}, u32[]{:S(2)}, u32[]{:S(2)}) collective-permute-start(f32[256,512]{1,0:T(8,128)S(1)} %get-tuple-element.41), channel_id=1, source_target_pairs={{0,1},{1,0},{2,3},{3,2},{4,5},{5,4},{6,7},{7,6},{8,9},{9,8},{10,11... | collective-permute-start | bytes 1572872 | tf_op jit(solution)/shard_map/ppermute | solution.py:269
  79.3 20.1 %copy-start.2 = (bf16[1,256,512]{2,1,0:T(8,128)(2,1)S(1)}, bf16[1,256,512]{2,1,0:T(8,128)(2,1)}, u32[]{:S(2)}) copy-start(bf16[1,256,512]{2,1,0:T(8,128)(2,1)} %param.9) | copy-start | bytes 786436
  79.3 20.1 %copy-start.7 = (f32[256,512]{1,0:T(8,128)S(1)}, f32[256,512]{1,0:T(8,128)}, u32[]{:S(2)}) copy-start(f32[256,512]{1,0:T(8,128)} %copy-done.6) | copy-start | bytes 1572868
  79.3 12.3 %collective-permute-start.10 = (s16[272,512]{1,0:T(8,128)(2,1)}, s16[272,512]{1,0:T(8,128)(2,1)S(1)}, u32[]{:S(2)}, u32[]{:S(2)}) collective-permute-start(s16[272,512]{1,0:T(8,128)(2,1)} %get-tuple-element.52), channel_id=1, source_target_pairs={{0,8},{1,25},{2,10},{3,27},{4,12},{5,29},{6,14},{7,31},{8,16},{9,1... | collective-permute-start | bytes 835592 | tf_op jit(solution)/shard_map/ppermute | solution.py:269
  81.9 17.4 %collective-permute-start.11 = (s16[272,512]{1,0:T(8,128)(2,1)}, s16[272,512]{1,0:T(8,128)(2,1)S(1)}, u32[]{:S(2)}, u32[]{:S(2)}) collective-permute-start(s16[272,512]{1,0:T(8,128)(2,1)} %get-tuple-element.53), channel_id=1, source_target_pairs={{0,24},{1,9},{2,26},{3,11},{4,28},{5,13},{6,30},{7,15},{8,0},{9,17... | collective-permute-start | bytes 835592 | tf_op jit(solution)/shard_map/ppermute | solution.py:269
  86.4 14.7 %collective-permute-start.6 = (f32[128,512]{1,0:T(8,128)}, f32[128,512]{1,0:T(8,128)S(1)}, u32[]{:S(2)}, u32[]{:S(2)}) collective-permute-start(f32[128,512]{1,0:T(8,128)} %get-tuple-element.43), channel_id=1, source_target_pairs={{0,2},{1,3},{2,0},{3,1},{4,6},{5,7},{6,4},{7,5},{8,10},{9,11},{10,... | collective-permute-start | bytes 786440 | tf_op jit(solution)/shard_map/ppermute | solution.py:269
  (6 other events, 6.1 us)
Sparse Core Ops, SparseCore 0:
  10.1 46.4 all-gather.2
